TPU v7x, 128 devices: a whole 4x4x4 slice. The times are simulated.
128 devices in a mesh: row: 8 (over y_hi, x), col: 16 (over y_lo, z, core).
Axes of the slice: x: 4, y: 4 (y_hi: 2, y_lo: 2; y = y_hi * 2 + y_lo), z: 4, core: 2. Of those that a mesh axis runs over, the one named last changes fastest.
Arguments:
- pair_in: bfloat16 [256, 256, 128], P('row', 'col'), may hold values from -6 to 6
- token_mask: int32 [256], replicated, may hold values 0 or 1
- cotangent: bfloat16 [256, 256, 128], P('row', 'col'), may hold values from -6 to 6
- gain_in: float32 [2, 128], replicated, may hold values from 0.1 to 1.9
- proj_w: bfloat16 [2, 128, 512], replicated, may hold values from -0.5 to 0.5
- gate_w: bfloat16 [2, 128, 128], replicated, may hold values from -0.5 to 0.5
- gain_mid: float32 [2, 128], replicated, may hold values from 0.1 to 1.9
- out_w: bfloat16 [2, 128, 128], replicated, may hold values from -0.5 to 0.5
Outputs:
- pair_out: bfloat16 [256, 256, 128], P('row', 'col')
- pair_grad: bfloat16 [256, 256, 128], P('row', 'col')
- gain_in_grad: float32 [2, 128], replicated
- proj_w_grad: float32 [2, 128, 512], replicated
- gate_w_grad: float32 [2, 128, 128], replicated
- gain_mid_grad: float32 [2, 128], replicated
- out_w_grad: float32 [2, 128, 128], replicated
Inputs may be any that keep to these rules, and one draw needn't show every extreme that they name: token_mask holds only 0 and 1.
All inputs are finite; a program needn't handle non-finite values.
Results may differ from a plain program's by a relative error of at most 0.023.
Values may be sent and summed in bfloat16 or wider, within the bound.
No kernel may reach another device: no remote copies, remote signals or barrier semaphores. Data moves between devices by JAX's collectives and lax.ppermute only.
A program may use at most 128 MiB of HBM per device.

v0:
```python
import functools

import jax
import jax.numpy as jnp
from jax import lax
from jax.experimental import pallas as pl
from jax.experimental.pallas import tpu as pltpu
from jax.sharding import PartitionSpec as P

F32 = jnp.float32
BF16 = jnp.bfloat16
C = 128
LANES = 128
ROWS = 32
COLS = 16
TOKENS = 256
PLACE = ROWS * COLS
TILES = PLACE // LANES
PEERS = 128
AXES = ("row", "col")
SUMS = 12


def mm(a, b, a_dim, b_dim):
    return lax.dot_general(
        a.astype(BF16), b.astype(BF16), (((a_dim,), (b_dim,)), ((), ())), preferred_element_type=F32
    )


def tile(t):
    return pl.ds(t * LANES, LANES)


def lane_index(rows):
    return lax.broadcasted_iota(jnp.int32, (rows, LANES), 1)


def swap_slots(parts):
    lane = lane_index(parts[0].shape[0])
    low = lane < 64
    even = (lane // 32) % 2 == 0
    turned = [pltpu.roll(part, 64, 1) for part in parts]
    first = [
        jnp.where(low, parts[0], turned[2]),
        jnp.where(low, parts[1], turned[3]),
        jnp.where(low, turned[0], parts[2]),
        jnp.where(low, turned[1], parts[3]),
    ]
    result = []
    for base in (0, 2):
        result.append(jnp.where(even, first[base], pltpu.roll(first[base + 1], 32, 1)))
        result.append(jnp.where(even, pltpu.roll(first[base], 96, 1), first[base + 1]))
    return result


def as_column(gain_ref, layer):
    return jnp.broadcast_to(gain_ref[pl.ds(layer, 1), :], (LANES, LANES)).T


def standardize(values):
    average = jnp.mean(values, axis=0, keepdims=True)
    centered = values - average
    variance = jnp.mean(centered * centered, axis=0, keepdims=True)
    scale = lax.rsqrt(variance + 1e-05)
    return centered * scale, scale


def standardize_back(d_unit, unit, scale):
    mean_d = jnp.mean(d_unit, axis=0, keepdims=True)
    mean_du = jnp.mean(d_unit * unit, axis=0, keepdims=True)
    return scale * (d_unit - mean_d - unit * mean_du)


def pairs_to_lanes(pairs_ref, spare):
    spare[...] = pairs_ref[...].astype(F32).reshape(PLACE, C)
    tiles = []
    for t in range(TILES):
        block = jnp.concatenate(
            [spare[pl.ds(4 * t + q, ROWS, COLS), :] for q in range(4)], axis=0
        )
        tiles.append(block.T)
    return tiles


def lanes_to_pairs(tiles, pairs_ref, spare):
    for t in range(TILES):
        block = tiles[t].T
        for q in range(4):
            spare[pl.ds(4 * t + q, ROWS, COLS), :] = block[q * ROWS : (q + 1) * ROWS, :]
    pairs_ref[...] = spare[...].reshape(ROWS, COLS, C).astype(pairs_ref.dtype)


def put_operands(t, left, right, spare):
    low = lane_index(C) < 64
    spare[pl.ds(2 * t, C, 8), :] = jnp.where(low, left, pltpu.roll(right, 64, 1))
    spare[pl.ds(2 * t + 1, C, 8), :] = jnp.where(low, pltpu.roll(left, 64, 1), right)


def get_operands(t, spare):
    low = lane_index(C) < 64
    even = spare[pl.ds(2 * t, C, 8), :]
    odd = spare[pl.ds(2 * t + 1, C, 8), :]
    left = jnp.where(low, even, pltpu.roll(odd, 64, 1))
    right = jnp.where(low, pltpu.roll(even, 64, 1), odd)
    return left, right


def front(tiles, gain, proj_t, gate_t, layer, spare, saved):
    unit_ref, scale_ref, normed_ref, fact_ref, gating_ref = saved
    for t, values in enumerate(tiles):
        unit, scale = standardize(values)
        unit_ref[:, tile(t)] = unit
        scale_ref[:, tile(t)] = jnp.broadcast_to(scale, (8, LANES))
        normed_ref[:, tile(t)] = (unit * gain).astype(BF16)
    normed = normed_ref[...]
    parts = []
    for base in (0, 2):
        closed = mm(proj_t[layer, pl.ds(base * C, C), :], normed, 1, 0)
        value = mm(proj_t[layer, pl.ds((base + 1) * C, C), :], normed, 1, 0)
        opened = jax.nn.sigmoid(closed)
        operand = opened * value
        fact_ref[pl.ds(base * C, C), :] = operand * (1.0 - opened)
        fact_ref[pl.ds((base + 1) * C, C), :] = opened
        parts.append(operand)
    for t in range(TILES):
        left, right = (part[:, t * LANES : (t + 1) * LANES] for part in parts)
        put_operands(t, left, right, spare)
    gating_ref[...] = jax.nn.sigmoid(mm(gate_t[layer], normed, 1, 0))


def ready_kernel(ready_ref):
    ready_ref[...] = jnp.zeros((8, LANES), F32)


def first_kernel(
    ready_ref, pair_ref, proj, gate, out_w, gin, gmid, tok,
    send_ref, unit_ref, scale_ref, normed_ref, fact_ref, gating_ref, x_ref,
    proj_out, gate_out, out_out, gin_out, gmid_out, tok_out, proj_t, gate_t, out_t,
    spare, pairs,
):
    for m in range(2):
        proj_t[m] = proj[m].T
        gate_t[m] = gate[m].T
        out_t[m] = out_w[m].T
    gain = as_column(gin, 0)
    tiles = pairs_to_lanes(pair_ref, pairs)
    saved = (unit_ref, scale_ref, normed_ref, fact_ref, gating_ref)
    for t in range(TILES):
        x_ref[:, tile(t)] = tiles[t].astype(BF16)
    front(tiles, gain, proj_t, gate_t, 0, spare, saved)
    send_ref[...] = spare[...].astype(BF16)
    for given, kept in (
        (proj, proj_out), (gate, gate_out), (out_w, out_out),
        (gin, gin_out), (gmid, gmid_out), (tok, tok_out),
    ):
        kept[...] = given[...]


def middle_kernel(
    mix_ref, x_ref, gating0_ref, gin, gmid, proj_t, gate_t, out_t,
    send_ref, unit_ref, scale_ref, normed_ref, fact_ref, gating_ref, next_ref,
    mix_unit_ref, mix_scale_ref, mix_normed_ref, gate_fact_ref, spare, mixed,
):
    mixed[...] = mix_ref[...].astype(F32)
    gain_a = as_column(gmid, 0)
    gain_b = as_column(gin, 1)
    saved = (unit_ref, scale_ref, normed_ref, fact_ref, gating_ref)
    for t in range(TILES):
        unit, scale = standardize(mixed[pl.ds(t, C, TILES), :])
        mix_unit_ref[:, tile(t)] = unit
        mix_scale_ref[:, tile(t)] = jnp.broadcast_to(scale, (8, LANES))
        mix_normed_ref[:, tile(t)] = (unit * gain_a).astype(BF16)
    update = mm(out_t[0], mix_normed_ref[...], 1, 0)
    tiles = []
    for t in range(TILES):
        gating = gating0_ref[:, tile(t)]
        gated = update[:, t * LANES : (t + 1) * LANES] * gating
        rounded = (x_ref[:, tile(t)].astype(F32) + gated).astype(BF16)
        next_ref[:, tile(t)] = rounded
        gate_fact_ref[:, tile(t)] = gated * (1.0 - gating)
        tiles.append(rounded.astype(F32))
    front(tiles, gain_b, proj_t, gate_t, 1, spare, saved)
    send_ref[...] = spare[...].astype(BF16)


def turn_kernel(
    mix_ref, x_ref, gating_ref, normed_ref, cot_ref, gmid, gate, out_w, out_t,
    pair_out_ref, send_ref, grad_ref, d_gated_ref, weights_ref,
    mixed, pairs, kept_n, kept_g, kept_d,
):
    mixed[...] = mix_ref[...].astype(F32)
    gain = as_column(gmid, 1)
    cot = pairs_to_lanes(cot_ref, pairs)
    units = []
    for t in range(TILES):
        units.append(standardize(mixed[pl.ds(t, C, TILES), :]))
        kept_n[:, tile(t)] = (units[t][0] * gain).astype(BF16)
        grad_ref[:, tile(t)] = cot[t]
        kept_d[:, tile(t)] = (cot[t] * gating_ref[:, tile(t)]).astype(BF16)
    d_normed = mm(out_w[1], kept_d[...], 1, 0)
    update = mm(out_t[1], kept_n[...], 1, 0)
    outs = []
    for t in range(TILES):
        piece = slice(t * LANES, (t + 1) * LANES)
        mixed[pl.ds(t, C, TILES), :] = standardize_back(d_normed[:, piece] * gain, *units[t])
        gating = gating_ref[:, tile(t)]
        gated = update[:, piece] * gating
        outs.append(x_ref[:, tile(t)].astype(F32) + gated)
        kept_g[:, tile(t)] = (cot[t] * gated * (1.0 - gating)).astype(BF16)
    d_gated_ref[...] = mm(gate[1], kept_g[...], 1, 0)
    send_ref[...] = mixed[...].astype(BF16)
    weights_ref[0] = mm(normed_ref[...], kept_g[...], 1, 1)
    weights_ref[1] = mm(kept_n[...], kept_d[...], 1, 1)
    lanes_to_pairs(outs, pair_out_ref, pairs)


def projected_back(t, spare, fact_ref, kept_p):
    d_left, d_right = get_operands(t, spare)
    for part, d_out in enumerate((d_left, d_left, d_right, d_right)):
        rows = pl.ds(part * C, C)
        kept_p[rows, tile(t)] = (d_out * fact_ref[rows, tile(t)]).astype(BF16)


def both_back_kernel(
    recv_ref, fact_ref, d_gated1_ref, unit_ref, scale_ref, grad_ref, normed1_ref, weights1_ref,
    gating_ref, mix_unit_ref, mix_scale_ref, mix_normed_ref, gate_fact_ref, normed0_ref,
    gin, gmid, proj, gate, out_w,
    send_ref, next_grad_ref, d_gated_ref, rows_ref,
    spare, mixed, kept_p, kept_g, kept_d,
):
    spare[...] = recv_ref[...].astype(F32)
    gain_a = as_column(gin, 1)
    gain_b = as_column(gmid, 0)
    for t in range(TILES):
        projected_back(t, spare, fact_ref, kept_p)
    d_normed = mm(proj[1], kept_p[...], 1, 0) + d_gated1_ref[...]
    for t in range(TILES):
        piece = slice(t * LANES, (t + 1) * LANES)
        d_x = standardize_back(
            d_normed[:, piece] * gain_a, unit_ref[:, tile(t)], scale_ref[pl.ds(0, 1), tile(t)]
        )
        grad = grad_ref[:, tile(t)] + d_x
        next_grad_ref[:, tile(t)] = grad
        kept_d[:, tile(t)] = (grad * gating_ref[:, tile(t)]).astype(BF16)
        kept_g[:, tile(t)] = (grad * gate_fact_ref[:, tile(t)]).astype(BF16)
    d_normed = mm(out_w[0], kept_d[...], 1, 0)
    for t in range(TILES):
        piece = slice(t * LANES, (t + 1) * LANES)
        mixed[pl.ds(t, C, TILES), :] = standardize_back(
            d_normed[:, piece] * gain_b,
            mix_unit_ref[:, tile(t)],
            mix_scale_ref[pl.ds(0, 1), tile(t)],
        )
    d_gated_ref[...] = mm(gate[0], kept_g[...], 1, 0)
    send_ref[...] = mixed[...].astype(BF16)
    first = mm(normed1_ref[...], kept_p[...], 1, 1)
    for e in range(4):
        rows_ref[pl.ds(4 + e, C, SUMS), :] = first[:, e * C : (e + 1) * C]
    rows_ref[pl.ds(8, C, SUMS), :] = mm(normed0_ref[...], kept_g[...], 1, 1)
    rows_ref[pl.ds(9, C, SUMS), :] = weights1_ref[0]
    rows_ref[pl.ds(10, C, SUMS), :] = mm(mix_normed_ref[...], kept_d[...], 1, 1)
    rows_ref[pl.ds(11, C, SUMS), :] = weights1_ref[1]


def last_back_kernel(
    recv_ref, fact_ref, normed_ref, rows_ref, d_gated_ref, unit_ref, scale_ref, grad_ref, gin, proj,
    send_ref, pair_grad_ref, spare, rows, kept_p, pairs,
):
    spare[...] = recv_ref[...].astype(F32)
    rows[...] = rows_ref[...]
    gain = as_column(gin, 0)
    outs = []
    for t in range(TILES):
        projected_back(t, spare, fact_ref, kept_p)
    d_normed = mm(proj[0], kept_p[...], 1, 0) + d_gated_ref[...]
    for t in range(TILES):
        d_x = standardize_back(
            d_normed[:, t * LANES : (t + 1) * LANES] * gain,
            unit_ref[:, tile(t)],
            scale_ref[pl.ds(0, 1), tile(t)],
        )
        outs.append(grad_ref[:, tile(t)] + d_x)
    weights = mm(normed_ref[...], kept_p[...], 1, 1)
    for e in range(4):
        rows[pl.ds(e, C, SUMS), :] = weights[:, e * C : (e + 1) * C]
    send_ref[...] = rows[...].astype(BF16)
    lanes_to_pairs(outs, pair_grad_ref, pairs)


def pair_mask(tok_ref):
    token = jnp.broadcast_to(tok_ref[...].astype(F32), (8, TOKENS))
    token = jnp.where(lax.broadcasted_iota(jnp.int32, (8, TOKENS), 0) == 0, token, 0.0)
    return mm(token, token, 0, 0)


def whole(spare, first):
    return jnp.concatenate([spare[first], spare[first + 1]], axis=1)


def product_kernel(layer, recv_ref, tok_ref, send_ref, left_ref, right_ref, spare):
    for hi in range(2):
        parts = [
            recv_ref[pl.ds((4 * hi + lo) * LANES, LANES), :] for lo in range(4)
        ]
        for slot, block in enumerate(swap_slots(parts)):
            spare[2 * (slot // 2) + hi, pl.ds(slot % 2, LANES, 2), :] = block.astype(F32)
    mask = pair_mask(tok_ref)
    left = (whole(spare, 0) * mask).astype(BF16)
    right = (whole(spare, 2) * mask).astype(BF16)
    left_ref[...] = left
    right_ref[...] = right
    mixture = mm(right, left, layer, layer)
    for hi in range(2):
        spare[hi] = mixture[:, hi * LANES : (hi + 1) * LANES]
    for hi in range(2):
        parts = [spare[hi, pl.ds(q, 64, 4), :].astype(BF16) for q in range(4)]
        for lo, block in enumerate(swap_slots(parts)):
            send_ref[pl.ds((4 * hi + lo) * 64, 64), :] = block


def product_back_kernel(
    layer, recv_ref, tok_ref, left_ref, right_ref, send_ref, spare
):
    for hi in range(2):
        parts = [recv_ref[pl.ds((4 * hi + lo) * 64, 64), :] for lo in range(4)]
        for q, block in enumerate(swap_slots(parts)):
            spare[hi, pl.ds(q, 64, 4), :] = block.astype(F32)
    d_mix = whole(spare, 0).astype(BF16)
    left = left_ref[...]
    right = right_ref[...]
    if layer == 0:
        d_left = mm(right, d_mix, 1, 0)
        d_right = mm(left, d_mix, 1, 1)
    else:
        d_left = mm(d_mix, right, 0, 0)
        d_right = mm(d_mix, left, 1, 0)
    mask = pair_mask(tok_ref)
    for first, value in ((0, d_left * mask), (2, d_right * mask)):
        for hi in range(2):
            spare[first + hi] = value[:, hi * LANES : (hi + 1) * LANES]
    for hi in range(2):
        parts = [
            spare[2 * (slot // 2) + hi, pl.ds(slot % 2, LANES, 2), :].astype(BF16)
            for slot in range(4)
        ]
        for lo, block in enumerate(swap_slots(parts)):
            send_ref[pl.ds((4 * hi + lo) * LANES, LANES), :] = block


def collect_kernel(recv_ref, send_ref):
    twice = jnp.sum(recv_ref[...].astype(F32).reshape(PEERS // 2, 2 * SUMS, LANES), axis=0)
    total = twice[0:SUMS] + twice[SUMS:]
    both = jnp.concatenate([total, total], axis=0)
    send_ref[...] = (
        jnp.broadcast_to(both[None], (PEERS // 2, 2 * SUMS, LANES))
        .reshape(PEERS * SUMS, LANES)
        .astype(BF16)
    )


def spread_kernel(
    recv_ref, out_ready, grad_ready, gin, gmid, proj, gate, out_w,
    pair_out_ref, pair_grad_ref, gin_ref, proj_ref, gate_ref, gmid_ref, out_ref,
    rows, gin_own, proj_own, gate_own, gmid_own, out_own, sems,
):
    copies = []

    def give(own, ref):
        copies.append(pltpu.make_async_copy(own, ref, sems.at[len(copies)]))
        copies[-1].start()

    give(out_ready, pair_out_ref)
    give(grad_ready, pair_grad_ref)
    rows[...] = recv_ref[...].astype(F32) * (1.0 / TOKENS)
    lane = lane_index(C)
    totals = jnp.zeros((C, LANES), F32)
    for m in range(2):
        gated = rows[pl.ds(8 + m, C, SUMS), :]
        mixed = rows[pl.ds(10 + m, C, SUMS), :]
        total = gated * gate[m].astype(F32)
        for e in range(4):
            part = rows[pl.ds(4 * m + e, C, SUMS), :]
            proj_own[m, :, tile(e)] = part
            total = total + part * proj[m, :, tile(e)].astype(F32)
        give(proj_own.at[m], proj_ref.at[m])
        gate_own[m] = gated
        out_own[m] = mixed
        total_in = jnp.sum(total, axis=1, keepdims=True)
        total_mid = jnp.sum(mixed * out_w[m].astype(F32), axis=1, keepdims=True)
        totals = jnp.where(lane == m, total_in, jnp.where(lane == 2 + m, total_mid, totals))
    give(gate_own, gate_ref)
    give(out_own, out_ref)
    turned = totals.T
    gin_own[...] = turned[0:2] / gin[...]
    gmid_own[...] = turned[2:4] / gmid[...]
    give(gin_own, gin_ref)
    give(gmid_own, gmid_ref)
    for copy in copies:
        copy.wait()


def run(kernel, outs, scratch, args, away=()):
    spaces = [pl.ANY if k in away else pltpu.VMEM for k in range(len(outs))]
    return pl.pallas_call(
        kernel,
        out_shape=[jax.ShapeDtypeStruct(shape, dtype) for shape, dtype in outs],
        in_specs=[pl.BlockSpec(memory_space=pltpu.VMEM)] * len(args),
        out_specs=[pl.BlockSpec(memory_space=space) for space in spaces],
        scratch_shapes=[
            pltpu.VMEM(shape, dtype) if shape else pltpu.SemaphoreType.DMA(dtype)
            for shape, dtype in scratch
        ],
        compiler_params=pltpu.CompilerParams(vmem_limit_bytes=16 * 1024 * 1024),
        cost_estimate=pl.CostEstimate(flops=10**9, bytes_accessed=2**20, transcendentals=2**18),
    )(*args)


def exchange(values, rows):
    return lax.all_to_all(
        values.reshape(-1, rows, LANES), AXES, 0, 0, tiled=True
    ).reshape(values.shape)


def local(pair_in, token_mask, cotangent, gain_in, proj_w, gate_w, gain_mid, out_w):
    operand = ((PEERS * 8, LANES), BF16)
    single = ((PEERS * 4, LANES), BF16)
    sums = (PEERS * SUMS, LANES)
    plane = ((C, PLACE), F32)
    plane_b = ((C, PLACE), BF16)
    four = (4 * C, PLACE)
    scales = ((8, PLACE), F32)
    square = ((TOKENS, TOKENS), BF16)
    spare = ((PEERS * 8, LANES), F32)
    pairs = ((PLACE, C), F32)
    mixed = ((PEERS * 4, LANES), F32)
    quarter = ((4, TOKENS, LANES), F32)
    pair_shape = ((ROWS, COLS, C), BF16)
    tok_in = token_mask.reshape(1, TOKENS)

    saved = [plane, scales, plane_b, (four, F32), plane, plane_b]
    (ready,) = run(ready_kernel, [((8, LANES), F32)], [], ())
    (
        send, unit0, scale0, normed0, fact0, gating0, x0,
        proj, gate, out, gin, gmid, tok, proj_t, gate_t, out_t,
    ) = run(
        first_kernel,
        [operand]
        + saved
        + [(a.shape, a.dtype) for a in (proj_w, gate_w, out_w, gain_in, gain_mid, tok_in)]
        + [((2, 4 * C, C), BF16), ((2, C, C), BF16), ((2, C, C), BF16)],
        [spare, pairs],
        (ready, pair_in, proj_w, gate_w, out_w, gain_in, gain_mid, tok_in),
    )
    send, left0, right0 = run(
        functools.partial(product_kernel, 0), [single, square, square], [quarter],
        (exchange(send, 8), tok),
    )
    (
        send, unit1, scale1, normed1, fact1, gating1, x1,
        mix_unit0, mix_scale0, mix_normed0, gate_fact0,
    ) = run(
        middle_kernel, [operand] + saved + [plane, scales, plane_b, plane], [spare, mixed],
        (exchange(send, 4), x0, gating0, gin, gmid, proj_t, gate_t, out_t),
    )
    send, left1, right1 = run(
        functools.partial(product_kernel, 1), [single, square, square], [quarter],
        (exchange(send, 8), tok),
    )
    ready_out, send, grad1, d_gated1, weights1 = run(
        turn_kernel, [pair_shape, single, plane, plane, ((2, C, C), F32)],
        [mixed, pairs, plane_b, plane_b, plane_b],
        (exchange(send, 4), x1, gating1, normed1, cotangent, gmid, gate, out, out_t),
    )
    (send,) = run(
        functools.partial(product_back_kernel, 1), [operand], [quarter],
        (exchange(send, 4), tok, left1, right1),
    )
    send, grad0, d_gated0, rows = run(
        both_back_kernel, [single, plane, plane, (sums, F32)],
        [spare, mixed, (four, BF16), plane_b, plane_b],
        (
            exchange(send, 8), fact1, d_gated1, unit1, scale1, grad1, normed1, weights1,
            gating0, mix_unit0, mix_scale0, mix_normed0, gate_fact0, normed0,
            gin, gmid, proj, gate, out,
        ),
    )
    (send,) = run(
        functools.partial(product_back_kernel, 0), [operand], [quarter],
        (exchange(send, 4), tok, left0, right0),
    )
    send, ready_grad = run(
        last_back_kernel, [(sums, BF16), pair_shape], [spare, (sums, F32), (four, BF16), pairs],
        (exchange(send, 8), fact0, normed0, rows, d_gated0, unit0, scale0, grad0, gin, proj),
    )
    (send,) = run(collect_kernel, [(sums, BF16)], [], (exchange(send, 4),))
    grads = [(a.shape, F32) for a in (gain_in, proj_w, gate_w, gain_mid, out_w)]
    pair_out, pair_grad, gin_grad, proj_grad, gate_grad, gmid_grad, out_grad = run(
        spread_kernel, [pair_shape] * 2 + grads, [(sums, F32)] + grads + [(None, (8,))],
        (exchange(send, 4), ready_out, ready_grad, gin, gmid, proj, gate, out),
        range(7),
    )
    return pair_out, pair_grad, gin_grad, proj_grad, gate_grad, gmid_grad, out_grad


def solution(mesh):
    placed = (P("row", "col", None), P(), P("row", "col", None), P(), P(), P(), P(), P())
    return jax.shard_map(
        local,
        mesh=mesh,
        in_specs=placed,
        out_specs=(P("row", "col", None), P("row", "col", None), P(), P(), P(), P(), P()),
        check_vma=False,
    )
```

profile of v0, /device:TPU:1, one launch (start us, length us, event | category | flops | bytes accessed | tf_op | source)
XLA Modules:
  0.0 166.6 jit_solution(12675135975297840697)
XLA Ops:
  0.6 0.0 copy-start.4
  0.6 0.0 copy-start.3
  0.7 0.0 copy-start
  0.7 0.0 copy-start.1
  0.7 0.0 copy-start.6
  0.7 0.0 copy-start.5
  0.7 0.8 copy-done.4
  1.5 0.0 copy-done.3
  1.5 0.2 copy-done
  1.7 0.0 copy-done.1
  1.7 0.7 shard_map.136
  2.4 22.8 %all_to_all.50 = bf16[128,8,128]{2,1,0:T(8,128)(2,1)S(1)} all-to-all(bf16[128,8,128]{2,1,0:T(8,128)(2,1)S(1)} %bitcast.26), channel_id=1, replica_groups=mesh['row'=8,'col'=16] {'row','col'}, dimensions={0} | all-to-all | bytes 524288 | tf_op jit(solution)/shard_map/all_to_all | solution.py:419
  25.2 0.7 shard_map.137
  25.8 14.1 %all_to_all.51 = bf16[128,4,128]{2,1,0:T(4,128)(2,1)S(1)} all-to-all(bf16[128,4,128]{2,1,0:T(4,128)(2,1)S(1)} %bitcast.38), channel_id=1, replica_groups=mesh['row'=8,'col'=16] {'row','col'}, dimensions={0} | all-to-all | bytes 262144 | tf_op jit(solution)/shard_map/all_to_all | solution.py:419
  39.9 0.9 shard_map.138
  40.8 15.0 %all_to_all.52 = bf16[128,8,128]{2,1,0:T(8,128)(2,1)S(1)} all-to-all(bf16[128,8,128]{2,1,0:T(8,128)(2,1)S(1)} %bitcast.27), channel_id=1, replica_groups=mesh['row'=8,'col'=16] {'row','col'}, dimensions={0} | all-to-all | bytes 524288 | tf_op jit(solution)/shard_map/all_to_all | solution.py:419
  55.8 0.6 shard_map.139
  56.5 0.0 copy-start.2
  56.5 14.1 %all_to_all.53 = bf16[128,4,128]{2,1,0:T(4,128)(2,1)S(1)} all-to-all(bf16[128,4,128]{2,1,0:T(4,128)(2,1)S(1)} %bitcast.39), channel_id=1, replica_groups=mesh['row'=8,'col'=16] {'row','col'}, dimensions={0} | all-to-all | bytes 262144 | tf_op jit(solution)/shard_map/all_to_all | solution.py:419
  70.6 0.8 shard_map.140
  71.4 14.0 %all_to_all.54 = bf16[128,4,128]{2,1,0:T(4,128)(2,1)S(1)} all-to-all(bf16[128,4,128]{2,1,0:T(4,128)(2,1)S(1)} %bitcast.36), channel_id=1, replica_groups=mesh['row'=8,'col'=16] {'row','col'}, dimensions={0} | all-to-all | bytes 262144 | tf_op jit(solution)/shard_map/all_to_all | solution.py:419
  85.3 0.7 shard_map.141
  86.0 15.0 %all_to_all.55 = bf16[128,8,128]{2,1,0:T(8,128)(2,1)S(1)} all-to-all(bf16[128,8,128]{2,1,0:T(8,128)(2,1)S(1)} %bitcast.32), channel_id=1, replica_groups=mesh['row'=8,'col'=16] {'row','col'}, dimensions={0} | all-to-all | bytes 524288 | tf_op jit(solution)/shard_map/all_to_all | solution.py:419
  101.1 1.0 shard_map.142
  102.1 14.1 %all_to_all.56 = bf16[128,4,128]{2,1,0:T(4,128)(2,1)S(1)} all-to-all(bf16[128,4,128]{2,1,0:T(4,128)(2,1)S(1)} %bitcast.33), channel_id=1, replica_groups=mesh['row'=8,'col'=16] {'row','col'}, dimensions={0} | all-to-all | bytes 262144 | tf_op jit(solution)/shard_map/all_to_all | solution.py:419
  116.2 0.6 shard_map.143
  116.9 15.0 %all_to_all.57 = bf16[128,8,128]{2,1,0:T(8,128)(2,1)S(1)} all-to-all(bf16[128,8,128]{2,1,0:T(8,128)(2,1)S(1)} %bitcast.31), channel_id=1, replica_groups=mesh['row'=8,'col'=16] {'row','col'}, dimensions={0} | all-to-all | bytes 524288 | tf_op jit(solution)/shard_map/all_to_all | solution.py:419
  131.9 0.7 shard_map.144
  132.6 16.5 %all_to_all.58 = bf16[384,4,128]{2,1,0:T(4,128)(2,1)S(1)} all-to-all(bf16[384,4,128]{2,1,0:T(4,128)(2,1)S(1)} %bitcast.23), channel_id=1, replica_groups=mesh['row'=8,'col'=16] {'row','col'}, dimensions={0} | all-to-all | bytes 786432 | tf_op jit(solution)/shard_map/all_to_all | solution.py:419
  149.1 0.1 shard_map.145
  149.2 16.4 %all_to_all.59 = bf16[384,4,128]{2,1,0:T(4,128)(2,1)S(1)} all-to-all(bf16[384,4,128]{2,1,0:T(4,128)(2,1)S(1)} %bitcast.25), channel_id=1, replica_groups=mesh['row'=8,'col'=16] {'row','col'}, dimensions={0} | all-to-all | bytes 786432 | tf_op jit(solution)/shard_map/all_to_all | solution.py:419
  165.6 1.1 shard_map.146
  (6 shorter events, 0.0 us)
Async XLA Ops:
  0.6 0.8 copy-start.4
  0.6 0.9 copy-start.3
  0.7 1.0 copy-start
  0.7 1.0 copy-start.1
  0.7 1.0 copy-start.6
  0.7 1.0 copy-start.7
  0.7 1.0 copy-start.5
  56.5 14.1 %copy-start.2 = (bf16[32,16,128]{2,1,0:T(8,128)(2,1)S(1)}, bf16[32,16,128]{2,1,0:T(8,128)(2,1)}, u32[]{:S(2)}) copy-start(bf16[32,16,128]{2,1,0:T(8,128)(2,1)} %cot_ref.1) | copy-start | bytes 393220
where the time goes:
time: 167 us
  blocking collectives  157 us (94%)
  Pallas kernels  7.87 us (5%)
    all_to_all x10, blocking collectives, exchange(): lax.all_to_all(values.reshape(-1, rows, LANES), AXES, 0, 0, tiled=True)  157 us
    pallas_call x12, Pallas kernels, run(): pl.pallas_call(kernel, out_shape=[jax.ShapeDtypeStruct(shape, dtype) for...  7.87 us

commit v1 on v0

v1 whole, which is shorter than its diff:
```python
import jax
import jax.numpy as jnp
from jax import lax
from jax.experimental import pallas as pl
from jax.experimental.pallas import tpu as pltpu
from jax.sharding import PartitionSpec as P

F32 = jnp.float32
BF16 = jnp.bfloat16
C = 128
LANES = 128
ROWS = 32
COLS = 16
TOKENS = 256
PLACE = ROWS * COLS
TILES = PLACE // LANES
PEERS = 128
AXES = ("row", "col")
SUMS = 12


def mm(a, b, a_dim, b_dim):
    return lax.dot_general(
        a.astype(BF16), b.astype(BF16), (((a_dim,), (b_dim,)), ((), ())), preferred_element_type=F32
    )


WIDE = PLACE // 2


def wide(h):
    return pl.ds(h * WIDE, WIDE)


def inner(h):
    return [(2 * h + k, slice(k * LANES, (k + 1) * LANES)) for k in range(2)]


def tile(t):
    return pl.ds(t * LANES, LANES)


def lane_index(rows):
    return lax.broadcasted_iota(jnp.int32, (rows, LANES), 1)


def swap_slots(parts):
    lane = lane_index(parts[0].shape[0])
    low = lane < 64
    even = (lane // 32) % 2 == 0
    turned = [pltpu.roll(part, 64, 1) for part in parts]
    first = [
        jnp.where(low, parts[0], turned[2]),
        jnp.where(low, parts[1], turned[3]),
        jnp.where(low, turned[0], parts[2]),
        jnp.where(low, turned[1], parts[3]),
    ]
    result = []
    for base in (0, 2):
        result.append(jnp.where(even, first[base], pltpu.roll(first[base + 1], 32, 1)))
        result.append(jnp.where(even, pltpu.roll(first[base], 96, 1), first[base + 1]))
    return result


def as_column(gain_ref, layer):
    return jnp.broadcast_to(gain_ref[pl.ds(layer, 1), :], (LANES, LANES)).T


def standardize(values):
    average = jnp.mean(values, axis=0, keepdims=True)
    centered = values - average
    variance = jnp.mean(centered * centered, axis=0, keepdims=True)
    scale = lax.rsqrt(variance + 1e-05)
    return centered * scale, scale


def standardize_back(d_unit, unit, scale):
    mean_d = jnp.mean(d_unit, axis=0, keepdims=True)
    mean_du = jnp.mean(d_unit * unit, axis=0, keepdims=True)
    return scale * (d_unit - mean_d - unit * mean_du)


def pairs_to_lanes(pairs_ref, spare):
    spare[...] = pairs_ref[...].astype(F32).reshape(PLACE, C)
    tiles = []
    for t in range(TILES):
        block = jnp.concatenate(
            [spare[pl.ds(4 * t + q, ROWS, COLS), :] for q in range(4)], axis=0
        )
        tiles.append(block.T)
    return tiles


def lanes_to_pairs(tiles, pairs_ref, spare):
    for t in range(TILES):
        block = tiles[t].T
        for q in range(4):
            spare[pl.ds(4 * t + q, ROWS, COLS), :] = block[q * ROWS : (q + 1) * ROWS, :]
    pairs_ref[...] = spare[...].reshape(ROWS, COLS, C).astype(pairs_ref.dtype)


def put_operands(t, left, right, spare):
    low = lane_index(C) < 64
    spare[pl.ds(2 * t, C, 8), :] = jnp.where(low, left, pltpu.roll(right, 64, 1))
    spare[pl.ds(2 * t + 1, C, 8), :] = jnp.where(low, pltpu.roll(left, 64, 1), right)


def get_operands(t, spare):
    low = lane_index(C) < 64
    even = spare[pl.ds(2 * t, C, 8), :]
    odd = spare[pl.ds(2 * t + 1, C, 8), :]
    left = jnp.where(low, even, pltpu.roll(odd, 64, 1))
    right = jnp.where(low, pltpu.roll(even, 64, 1), odd)
    return left, right


def front(h, tiles, gain, proj_t, gate_t, layer, spare, saved, valid):
    unit_ref, scale_ref, normed_ref, fact_ref, gating_ref = saved
    for (t, _), values in zip(inner(h), tiles):
        unit, scale = standardize(values)
        unit_ref[:, tile(t)] = unit
        scale_ref[:, tile(t)] = jnp.broadcast_to(scale, (8, LANES))
        normed_ref[:, tile(t)] = (unit * gain).astype(BF16)
    normed = normed_ref[:, wide(h)]
    parts = []
    for base in (0, 2):
        closed = mm(proj_t[layer, pl.ds(base * C, C), :], normed, 1, 0)
        value = mm(proj_t[layer, pl.ds((base + 1) * C, C), :], normed, 1, 0)
        opened = jax.nn.sigmoid(closed)
        operand = opened * value * valid
        fact_ref[pl.ds(base * C, C), wide(h)] = operand * (1.0 - opened)
        fact_ref[pl.ds((base + 1) * C, C), wide(h)] = opened * valid
        parts.append(operand)
    for t, piece in inner(h):
        put_operands(t, parts[0][:, piece], parts[1][:, piece], spare)
    gating_ref[:, wide(h)] = jax.nn.sigmoid(mm(gate_t[layer], normed, 1, 0))


def place_kernel(first_ref, second_ref):
    token = lax.broadcasted_iota(jnp.int32, (TOKENS, PLACE), 0)
    place = lax.broadcasted_iota(jnp.int32, (TOKENS, PLACE), 1)
    first = place % ROWS + ROWS * lax.axis_index("row")
    second = place // ROWS + COLS * lax.axis_index("col")
    first_ref[...] = (token == first).astype(F32).astype(BF16)
    second_ref[...] = (token == second).astype(F32).astype(BF16)


def first_kernel(
    first_ref, second_ref, tok, pair_ref, proj, gate, out_w, gin, gmid,
    send_ref, unit_ref, scale_ref, normed_ref, fact_ref, gating_ref, x_ref,
    proj_out, gate_out, out_out, gin_out, gmid_out, proj_t, gate_t, out_t,
    valid_ref, spare, pairs,
):
    token = jnp.broadcast_to(tok[...].astype(F32), (8, TOKENS))
    valid_ref[...] = mm(token, first_ref[...], 1, 0) * mm(token, second_ref[...], 1, 0)
    for m in range(2):
        proj_t[m] = proj[m].T
        gate_t[m] = gate[m].T
        out_t[m] = out_w[m].T
    gain = as_column(gin, 0)
    tiles = pairs_to_lanes(pair_ref, pairs)
    saved = (unit_ref, scale_ref, normed_ref, fact_ref, gating_ref)
    for t in range(TILES):
        x_ref[:, tile(t)] = tiles[t].astype(BF16)
    for h in range(2):
        valid = valid_ref[pl.ds(0, 1), wide(h)]
        front(h, tiles[2 * h : 2 * h + 2], gain, proj_t, gate_t, 0, spare, saved, valid)
    send_ref[...] = spare[...].astype(BF16)
    for given, kept in (
        (proj, proj_out), (gate, gate_out), (out_w, out_out),
        (gin, gin_out), (gmid, gmid_out),
    ):
        kept[...] = given[...]


def middle_kernel(
    mix_ref, x_ref, gating0_ref, valid_ref, gin, gmid, proj_t, gate_t, out_t,
    send_ref, unit_ref, scale_ref, normed_ref, fact_ref, gating_ref, next_ref,
    mix_unit_ref, mix_scale_ref, mix_normed_ref, gate_fact_ref, spare, mixed,
):
    mixed[...] = mix_ref[...].astype(F32)
    gain_a = as_column(gmid, 0)
    gain_b = as_column(gin, 1)
    saved = (unit_ref, scale_ref, normed_ref, fact_ref, gating_ref)
    updates = []
    for h in range(2):
        for t, _ in inner(h):
            unit, scale = standardize(mixed[pl.ds(t, C, TILES), :])
            mix_unit_ref[:, tile(t)] = unit
            mix_scale_ref[:, tile(t)] = jnp.broadcast_to(scale, (8, LANES))
            mix_normed_ref[:, tile(t)] = (unit * gain_a).astype(BF16)
        updates.append(mm(out_t[0], mix_normed_ref[:, wide(h)], 1, 0))
    for h in range(2):
        tiles = []
        for t, piece in inner(h):
            gating = gating0_ref[:, tile(t)]
            gated = updates[h][:, piece] * gating
            rounded = (x_ref[:, tile(t)].astype(F32) + gated).astype(BF16)
            next_ref[:, tile(t)] = rounded
            gate_fact_ref[:, tile(t)] = gated * (1.0 - gating)
            tiles.append(rounded.astype(F32))
        valid = valid_ref[pl.ds(0, 1), wide(h)]
        front(h, tiles, gain_b, proj_t, gate_t, 1, spare, saved, valid)
    send_ref[...] = spare[...].astype(BF16)


def turn_kernel(
    mix_ref, x_ref, gating_ref, normed_ref, cot_ref, gmid, gate, out_w, out_t,
    pair_out_ref, send_ref, grad_ref, d_gated_ref, weights_ref,
    mixed, pairs, kept_n, kept_g, kept_d,
):
    mixed[...] = mix_ref[...].astype(F32)
    gain = as_column(gmid, 1)
    cot = pairs_to_lanes(cot_ref, pairs)
    units, d_normed, update = [], [], []
    for h in range(2):
        for t, _ in inner(h):
            units.append(standardize(mixed[pl.ds(t, C, TILES), :]))
            kept_n[:, tile(t)] = (units[t][0] * gain).astype(BF16)
            grad_ref[:, tile(t)] = cot[t]
            kept_d[:, tile(t)] = (cot[t] * gating_ref[:, tile(t)]).astype(BF16)
        d_normed.append(mm(out_w[1], kept_d[:, wide(h)], 1, 0))
        update.append(mm(out_t[1], kept_n[:, wide(h)], 1, 0))
    outs = []
    for h in range(2):
        for t, piece in inner(h):
            mixed[pl.ds(t, C, TILES), :] = standardize_back(d_normed[h][:, piece] * gain, *units[t])
            gating = gating_ref[:, tile(t)]
            gated = update[h][:, piece] * gating
            outs.append(x_ref[:, tile(t)].astype(F32) + gated)
            kept_g[:, tile(t)] = (cot[t] * gated * (1.0 - gating)).astype(BF16)
    d_gated_ref[...] = mm(gate[1], kept_g[...], 1, 0)
    send_ref[...] = mixed[...].astype(BF16)
    weights_ref[0] = mm(normed_ref[...], kept_g[...], 1, 1)
    weights_ref[1] = mm(kept_n[...], kept_d[...], 1, 1)
    lanes_to_pairs(outs, pair_out_ref, pairs)


def projected_back(t, spare, fact_ref, kept_p):
    d_left, d_right = get_operands(t, spare)
    for part, d_out in enumerate((d_left, d_left, d_right, d_right)):
        rows = pl.ds(part * C, C)
        kept_p[rows, tile(t)] = (d_out * fact_ref[rows, tile(t)]).astype(BF16)


def both_back_kernel(
    recv_ref, fact_ref, d_gated1_ref, unit_ref, scale_ref, grad_ref, normed1_ref, weights1_ref,
    gating_ref, mix_unit_ref, mix_scale_ref, mix_normed_ref, gate_fact_ref, normed0_ref,
    gin, gmid, proj, gate, out_w, out_ready,
    send_ref, next_grad_ref, d_gated_ref, keep_ref, pair_out_ref,
    spare, kept_p, kept_g, kept_d, sem,
):
    copy = pltpu.make_async_copy(out_ready, pair_out_ref, sem)
    copy.start()
    spare[...] = recv_ref[...].astype(F32)
    gain_a = as_column(gin, 1)
    gain_b = as_column(gmid, 0)
    d_normed = []
    for h in range(2):
        for t, _ in inner(h):
            projected_back(t, spare, fact_ref, kept_p)
        d_normed.append(mm(proj[1], kept_p[:, wide(h)], 1, 0) + d_gated1_ref[:, wide(h)])
    d_mid = []
    for h in range(2):
        for t, piece in inner(h):
            d_x = standardize_back(
                d_normed[h][:, piece] * gain_a,
                unit_ref[:, tile(t)],
                scale_ref[pl.ds(0, 1), tile(t)],
            )
            grad = grad_ref[:, tile(t)] + d_x
            next_grad_ref[:, tile(t)] = grad
            kept_d[:, tile(t)] = (grad * gating_ref[:, tile(t)]).astype(BF16)
            kept_g[:, tile(t)] = (grad * gate_fact_ref[:, tile(t)]).astype(BF16)
        d_mid.append(mm(out_w[0], kept_d[:, wide(h)], 1, 0))
    weights = mm(normed1_ref[...], kept_p[...], 1, 1)
    for h in range(2):
        for t, piece in inner(h):
            spare[pl.ds(t, C, 8), :] = standardize_back(
                d_mid[h][:, piece] * gain_b,
                mix_unit_ref[:, tile(t)],
                mix_scale_ref[pl.ds(0, 1), tile(t)],
            )
            spare[pl.ds(TILES + t, C, 8), :] = weights[:, t * LANES : (t + 1) * LANES]
    d_gated_ref[...] = mm(gate[0], kept_g[...], 1, 0)
    send_ref[...] = spare[...].astype(BF16)
    keep_ref[0] = mm(normed0_ref[...], kept_g[...], 1, 1)
    keep_ref[1] = weights1_ref[0]
    keep_ref[2] = mm(mix_normed_ref[...], kept_d[...], 1, 1)
    keep_ref[3] = weights1_ref[1]
    copy.wait()


def last_back_kernel(
    recv_ref, fact_ref, normed_ref, keep_ref, d_gated_ref, unit_ref, scale_ref, grad_ref, gin, proj,
    send_ref, pair_grad_ref, spare, kept_p, pairs,
):
    spare[...] = recv_ref[...].astype(F32)
    gain = as_column(gin, 0)
    outs = []
    d_normed = []
    for h in range(2):
        for t, _ in inner(h):
            projected_back(t, spare, fact_ref, kept_p)
        d_normed.append(mm(proj[0], kept_p[:, wide(h)], 1, 0) + d_gated_ref[:, wide(h)])
    for h in range(2):
        for t, piece in inner(h):
            d_x = standardize_back(
                d_normed[h][:, piece] * gain,
                unit_ref[:, tile(t)],
                scale_ref[pl.ds(0, 1), tile(t)],
            )
            outs.append(grad_ref[:, tile(t)] + d_x)
    weights = mm(normed_ref[...], kept_p[...], 1, 1)
    for e in range(4):
        spare[pl.ds(e, C, 8), :] = weights[:, e * C : (e + 1) * C]
        spare[pl.ds(4 + e, C, 8), :] = keep_ref[e]
    send_ref[...] = spare[...].astype(BF16)
    lanes_to_pairs(outs, pair_grad_ref, pairs)


def whole(spare, first):
    return jnp.concatenate([spare[first], spare[first + 1]], axis=1)


def halves(hi, q):
    return pl.ds(q * LANES, LANES), tile(hi)


def second_rows(layer, q):
    return pl.ds(q, 64, 4) if layer == 0 else pl.ds((q % 2) * LANES + q // 2, 64, 2)


def take_operands(recv_ref, put):
    for hi in range(2):
        parts = [recv_ref[pl.ds((4 * hi + lo) * LANES, LANES), :] for lo in range(4)]
        for slot, block in enumerate(swap_slots(parts)):
            put(hi, slot, block)


def send_operands(send_ref, get):
    for hi in range(2):
        parts = [get(hi, slot) for slot in range(4)]
        for lo, block in enumerate(swap_slots(parts)):
            send_ref[pl.ds((4 * hi + lo) * LANES, LANES), :] = block


def send_mixture(layer, mixture, send_ref, spare):
    for hi in range(2):
        spare[hi] = mixture(hi)
    for hi in range(2):
        parts = [spare[hi, second_rows(layer, q), :].astype(BF16) for q in range(4)]
        for lo, block in enumerate(swap_slots(parts)):
            send_ref[pl.ds((4 * hi + lo) * 64, 64), :] = block


def outgoing_kernel(recv_ref, send_ref, left_ref, right_ref, spare):
    def put(hi, slot, block):
        (left_ref if slot < 2 else right_ref)[halves(hi, slot % 2)] = block

    take_operands(recv_ref, put)
    right = right_ref[...]
    send_mixture(0, lambda hi: mm(right, left_ref[:, tile(hi)], 0, 0), send_ref, spare)


def incoming_kernel(recv_ref, send_ref, left_ref, right_ref, spare):
    def put(hi, slot, block):
        if slot < 2:
            spare[hi, pl.ds(slot, LANES, 2), :] = block.astype(F32)
        else:
            right_ref[halves(hi, slot % 2)] = block

    take_operands(recv_ref, put)
    left = whole(spare, 0).astype(BF16)
    left_ref[...] = left
    mixture = mm(right_ref[...], left, 1, 1)
    send_mixture(1, lambda hi: mixture[:, hi * LANES : (hi + 1) * LANES], send_ref, spare)


def incoming_back_kernel(recv_ref, left_ref, right_ref, send_ref, spare, d_rows):
    for hi in range(2):
        parts = [recv_ref[pl.ds((4 * hi + lo) * 64, 64), :] for lo in range(4)]
        for q, block in enumerate(swap_slots(parts)):
            spare[hi, second_rows(1, q), :] = block.astype(F32)
    d_mix = whole(spare, 0).astype(BF16)
    d_left = mm(d_mix, right_ref[...], 0, 0)
    d_rows[...] = mm(d_mix, left_ref[...], 1, 0).astype(BF16)
    for hi in range(2):
        spare[hi] = d_left[:, hi * LANES : (hi + 1) * LANES]

    def get(hi, slot):
        if slot < 2:
            return spare[hi, pl.ds(slot, LANES, 2), :].astype(BF16)
        return d_rows[halves(hi, slot % 2)]

    send_operands(send_ref, get)


def outgoing_back_kernel(
    recv_ref, left_ref, right_ref, send_ref, sums_ref, arrived, spare, d_rows
):
    arrived[...] = recv_ref[...].astype(F32)
    for hi in range(2):
        parts = [
            jnp.concatenate(
                [arrived[pl.ds((4 * hi + lo) * LANES + jm, COLS, 8), :] for jm in range(4)], axis=0
            ).astype(BF16)
            for lo in range(4)
        ]
        for q, block in enumerate(swap_slots(parts)):
            for jm in range(4):
                spare[hi, pl.ds(4 * jm + q, COLS, COLS), :] = block[
                    jm * COLS : (jm + 1) * COLS, :
                ].astype(F32)
    d_mix = whole(spare, 0).astype(BF16)
    d_rows[0] = mm(right_ref[...], d_mix, 1, 0).astype(BF16)
    d_rows[1] = mm(left_ref[...], d_mix, 1, 1).astype(BF16)

    def get(hi, slot):
        rows, lanes = halves(hi, slot % 2)
        return d_rows[slot // 2, rows, lanes]

    send_operands(send_ref, get)
    total = jnp.sum(recv_ref[...].astype(F32).reshape(PEERS, 8, LANES), axis=0)
    sums_ref[...] = total[TILES:]


def collect_kernel(recv_ref, sums_ref, send_ref):
    total = jnp.sum(recv_ref[...].astype(F32).reshape(PEERS, 8, LANES), axis=0)
    block = [total[0:4], sums_ref[...], total[4:8]]
    both = jnp.concatenate(block + block, axis=0)
    send_ref[...] = (
        jnp.broadcast_to(both[None], (PEERS // 2, 2 * SUMS, LANES))
        .reshape(PEERS * SUMS, LANES)
        .astype(BF16)
    )


def spread_kernel(
    recv_ref, grad_ready, gin, gmid, proj, gate, out_w,
    pair_grad_ref, gin_ref, proj_ref, gate_ref, gmid_ref, out_ref,
    rows, gin_own, proj_own, gate_own, gmid_own, out_own, sems,
):
    copies = []

    def give(own, ref):
        copies.append(pltpu.make_async_copy(own, ref, sems.at[len(copies)]))
        copies[-1].start()

    give(grad_ready, pair_grad_ref)
    rows[...] = recv_ref[...].astype(F32) * (1.0 / TOKENS)
    lane = lane_index(C)
    totals = jnp.zeros((C, LANES), F32)
    for m in range(2):
        gated = rows[pl.ds(8 + m, C, SUMS), :]
        mixed = rows[pl.ds(10 + m, C, SUMS), :]
        total = gated * gate[m].astype(F32)
        for e in range(4):
            part = rows[pl.ds(4 * m + e, C, SUMS), :]
            proj_own[m, :, tile(e)] = part
            total = total + part * proj[m, :, tile(e)].astype(F32)
        give(proj_own.at[m], proj_ref.at[m])
        gate_own[m] = gated
        out_own[m] = mixed
        total_in = jnp.sum(total, axis=1, keepdims=True)
        total_mid = jnp.sum(mixed * out_w[m].astype(F32), axis=1, keepdims=True)
        totals = jnp.where(lane == m, total_in, jnp.where(lane == 2 + m, total_mid, totals))
    give(gate_own, gate_ref)
    give(out_own, out_ref)
    turned = totals.T
    gin_own[...] = turned[0:2] / gin[...]
    gmid_own[...] = turned[2:4] / gmid[...]
    give(gin_own, gin_ref)
    give(gmid_own, gmid_ref)
    for copy in copies:
        copy.wait()


def run(kernel, outs, scratch, args, away=()):
    spaces = [pl.ANY if k in away else pltpu.VMEM for k in range(len(outs))]
    return pl.pallas_call(
        kernel,
        out_shape=[jax.ShapeDtypeStruct(shape, dtype) for shape, dtype in outs],
        in_specs=[pl.BlockSpec(memory_space=pltpu.VMEM)] * len(args),
        out_specs=[pl.BlockSpec(memory_space=space) for space in spaces],
        scratch_shapes=[
            pltpu.VMEM(shape, dtype) if shape else pltpu.SemaphoreType.DMA(dtype)
            for shape, dtype in scratch
        ],
        compiler_params=pltpu.CompilerParams(vmem_limit_bytes=16 * 1024 * 1024),
        cost_estimate=pl.CostEstimate(flops=10**9, bytes_accessed=2**20, transcendentals=2**18),
    )(*args)


def exchange(values, rows):
    return lax.all_to_all(
        values.reshape(-1, rows, LANES), AXES, 0, 0, tiled=True
    ).reshape(values.shape)


def local(pair_in, token_mask, cotangent, gain_in, proj_w, gate_w, gain_mid, out_w):
    operand = ((PEERS * 8, LANES), BF16)
    single = ((PEERS * 4, LANES), BF16)
    sums = (PEERS * SUMS, LANES)
    plane = ((C, PLACE), F32)
    plane_b = ((C, PLACE), BF16)
    four = (4 * C, PLACE)
    scales = ((8, PLACE), F32)
    square = ((TOKENS, TOKENS), BF16)
    spare = ((PEERS * 8, LANES), F32)
    pairs = ((PLACE, C), F32)
    mixed = ((PEERS * 4, LANES), F32)
    half = ((2, TOKENS, LANES), F32)
    pair_shape = ((ROWS, COLS, C), BF16)

    saved = [plane, scales, plane_b, (four, F32), plane, plane_b]
    places = run(place_kernel, [((TOKENS, PLACE), BF16)] * 2, [], ())
    (
        send, unit0, scale0, normed0, fact0, gating0, x0,
        proj, gate, out, gin, gmid, proj_t, gate_t, out_t, valid,
    ) = run(
        first_kernel,
        [operand]
        + saved
        + [(a.shape, a.dtype) for a in (proj_w, gate_w, out_w, gain_in, gain_mid)]
        + [((2, 4 * C, C), BF16), ((2, C, C), BF16), ((2, C, C), BF16)]
        + [scales],
        [spare, pairs],
        (
            *places, token_mask.reshape(1, TOKENS), pair_in,
            proj_w, gate_w, out_w, gain_in, gain_mid,
        ),
    )
    send, left0, right0 = run(outgoing_kernel, [single, square, square], [half], (exchange(send, 8),))
    (
        send, unit1, scale1, normed1, fact1, gating1, x1,
        mix_unit0, mix_scale0, mix_normed0, gate_fact0,
    ) = run(
        middle_kernel, [operand] + saved + [plane, scales, plane_b, plane], [spare, mixed],
        (exchange(send, 4), x0, gating0, valid, gin, gmid, proj_t, gate_t, out_t),
    )
    send, left1, right1 = run(
        incoming_kernel, [single, square, square], [half], (exchange(send, 8),)
    )
    ready_out, send, grad1, d_gated1, weights1 = run(
        turn_kernel, [pair_shape, single, plane, plane, ((2, C, C), F32)],
        [mixed, pairs, plane_b, plane_b, plane_b],
        (exchange(send, 4), x1, gating1, normed1, cotangent, gmid, gate, out, out_t),
    )
    (send,) = run(
        incoming_back_kernel, [operand], [half, square],
        (exchange(send, 4), left1, right1),
    )
    send, grad0, d_gated0, keep, pair_out = run(
        both_back_kernel, [operand, plane, plane, ((4, C, C), F32), pair_shape],
        [spare, (four, BF16), plane_b, plane_b, (None, ())],
        (
            exchange(send, 8), fact1, d_gated1, unit1, scale1, grad1, normed1, weights1,
            gating0, mix_unit0, mix_scale0, mix_normed0, gate_fact0, normed0,
            gin, gmid, proj, gate, out, ready_out,
        ),
        (4,),
    )
    send, sums1 = run(
        outgoing_back_kernel, [operand, ((4, LANES), F32)],
        [spare, half, ((2, TOKENS, TOKENS), BF16)],
        (exchange(send, 8), left0, right0),
    )
    send, ready_grad = run(
        last_back_kernel, [operand, pair_shape], [spare, (four, BF16), pairs],
        (exchange(send, 8), fact0, normed0, keep, d_gated0, unit0, scale0, grad0, gin, proj),
    )
    (send,) = run(collect_kernel, [(sums, BF16)], [], (exchange(send, 8), sums1))
    grads = [(a.shape, F32) for a in (gain_in, proj_w, gate_w, gain_mid, out_w)]
    pair_grad, gin_grad, proj_grad, gate_grad, gmid_grad, out_grad = run(
        spread_kernel, [pair_shape] + grads, [(sums, F32)] + grads + [(None, (7,))],
        (exchange(send, 4), ready_grad, gin, gmid, proj, gate, out),
        range(6),
    )
    return pair_out, pair_grad, gin_grad, proj_grad, gate_grad, gmid_grad, out_grad


def solution(mesh):
    placed = (P("row", "col", None), P(), P("row", "col", None), P(), P(), P(), P(), P())
    return jax.shard_map(
        local,
        mesh=mesh,
        in_specs=placed,
        out_specs=(P("row", "col", None), P("row", "col", None), P(), P(), P(), P(), P()),
        check_vma=False,
    )
```

time: 167 us -> 167 us (level)
  no operation moved by 1% of the time
where the time goes in v1:
time: 167 us; the launch traced here: 166 us
  blocking collectives  157 us (94%)
  Pallas kernels  7.85 us (5%)
    all_to_all x10, blocking collectives, exchange(): lax.all_to_all(values.reshape(-1, rows, LANES), AXES, 0, 0, tiled=True)  157 us
    pallas_call x12, Pallas kernels, run(): pl.pallas_call(kernel, out_shape=[jax.ShapeDtypeStruct(shape, dtype) for...  7.85 us

profile of v1, /device:TPU:1, one launch (start us, length us, event | category | flops | bytes accessed | tf_op | source)
XLA Modules:
  0.0 166.4 jit_solution(6544851638602470832)
XLA Ops:
  0.6 0.0 copy-start.4
  0.6 0.0 copy-start.3
  0.7 0.0 copy-start
  0.7 0.0 copy-start.1
  0.7 0.1 shard_map.135
  0.8 0.0 copy-start.5
  0.8 0.7 copy-done.4
  1.5 0.0 copy-done.3
  1.5 0.2 copy-done
  1.7 0.0 copy-done.1
  1.7 0.7 shard_map.136
  2.4 22.8 %all_to_all.50 = bf16[128,8,128]{2,1,0:T(8,128)(2,1)S(1)} all-to-all(bf16[128,8,128]{2,1,0:T(8,128)(2,1)S(1)} %bitcast.25), channel_id=1, replica_groups=mesh['row'=8,'col'=16] {'row','col'}, dimensions={0} | all-to-all | bytes 524288 | tf_op jit(solution)/shard_map/all_to_all | solution.py:496
  25.1 0.6 shard_map.137
  25.7 14.1 %all_to_all.51 = bf16[128,4,128]{2,1,0:T(4,128)(2,1)S(1)} all-to-all(bf16[128,4,128]{2,1,0:T(4,128)(2,1)S(1)} %bitcast.38), channel_id=1, replica_groups=mesh['row'=8,'col'=16] {'row','col'}, dimensions={0} | all-to-all | bytes 262144 | tf_op jit(solution)/shard_map/all_to_all | solution.py:496
  39.9 0.9 shard_map.138
  40.7 15.0 %all_to_all.52 = bf16[128,8,128]{2,1,0:T(8,128)(2,1)S(1)} all-to-all(bf16[128,8,128]{2,1,0:T(8,128)(2,1)S(1)} %bitcast.26), channel_id=1, replica_groups=mesh['row'=8,'col'=16] {'row','col'}, dimensions={0} | all-to-all | bytes 524288 | tf_op jit(solution)/shard_map/all_to_all | solution.py:496
  55.7 0.6 shard_map.139
  56.3 0.0 copy-start.2
  56.4 14.1 %all_to_all.53 = bf16[128,4,128]{2,1,0:T(4,128)(2,1)S(1)} all-to-all(bf16[128,4,128]{2,1,0:T(4,128)(2,1)S(1)} %bitcast.39), channel_id=1, replica_groups=mesh['row'=8,'col'=16] {'row','col'}, dimensions={0} | all-to-all | bytes 262144 | tf_op jit(solution)/shard_map/all_to_all | solution.py:496
  70.5 0.7 shard_map.140
  71.2 14.0 %all_to_all.54 = bf16[128,4,128]{2,1,0:T(4,128)(2,1)S(1)} all-to-all(bf16[128,4,128]{2,1,0:T(4,128)(2,1)S(1)} %bitcast.37), channel_id=1, replica_groups=mesh['row'=8,'col'=16] {'row','col'}, dimensions={0} | all-to-all | bytes 262144 | tf_op jit(solution)/shard_map/all_to_all | solution.py:496
  85.2 0.6 shard_map.141
  85.8 15.0 %all_to_all.55 = bf16[128,8,128]{2,1,0:T(8,128)(2,1)S(1)} all-to-all(bf16[128,8,128]{2,1,0:T(8,128)(2,1)S(1)} %bitcast.33), channel_id=1, replica_groups=mesh['row'=8,'col'=16] {'row','col'}, dimensions={0} | all-to-all | bytes 524288 | tf_op jit(solution)/shard_map/all_to_all | solution.py:496
  100.8 1.1 shard_map.142
  101.9 15.1 %all_to_all.56 = bf16[128,8,128]{2,1,0:T(8,128)(2,1)S(1)} all-to-all(bf16[128,8,128]{2,1,0:T(8,128)(2,1)S(1)} %bitcast.24), channel_id=1, replica_groups=mesh['row'=8,'col'=16] {'row','col'}, dimensions={0} | all-to-all | bytes 524288 | tf_op jit(solution)/shard_map/all_to_all | solution.py:496
  117.0 0.7 shard_map.143
  117.7 15.1 %all_to_all.57 = bf16[128,8,128]{2,1,0:T(8,128)(2,1)S(1)} all-to-all(bf16[128,8,128]{2,1,0:T(8,128)(2,1)S(1)} %bitcast.30), channel_id=1, replica_groups=mesh['row'=8,'col'=16] {'row','col'}, dimensions={0} | all-to-all | bytes 524288 | tf_op jit(solution)/shard_map/all_to_all | solution.py:496
  132.8 0.8 shard_map.144
  133.6 15.1 %all_to_all.58 = bf16[128,8,128]{2,1,0:T(8,128)(2,1)S(1)} all-to-all(bf16[128,8,128]{2,1,0:T(8,128)(2,1)S(1)} %bitcast.28), channel_id=1, replica_groups=mesh['row'=8,'col'=16] {'row','col'}, dimensions={0} | all-to-all | bytes 524288 | tf_op jit(solution)/shard_map/all_to_all | solution.py:496
  148.8 0.2 shard_map.145
  148.9 16.5 %all_to_all.59 = bf16[384,4,128]{2,1,0:T(4,128)(2,1)S(1)} all-to-all(bf16[384,4,128]{2,1,0:T(4,128)(2,1)S(1)} %bitcast.23), channel_id=1, replica_groups=mesh['row'=8,'col'=16] {'row','col'}, dimensions={0} | all-to-all | bytes 786432 | tf_op jit(solution)/shard_map/all_to_all | solution.py:496
  165.4 1.1 shard_map.146
  (6 shorter events, 0.0 us)
Async XLA Ops:
  0.6 0.8 copy-start.4
  0.6 0.9 copy-start.3
  0.7 1.0 copy-start
  0.7 1.0 copy-start.1
  0.7 1.0 copy-start.6
  0.7 1.0 copy-start.7
  0.8 0.9 copy-start.5
  56.3 14.1 %copy-start.2 = (bf16[32,16,128]{2,1,0:T(8,128)(2,1)S(1)}, bf16[32,16,128]{2,1,0:T(8,128)(2,1)}, u32[]{:S(2)}) copy-start(bf16[32,16,128]{2,1,0:T(8,128)(2,1)} %cot_ref.1) | copy-start | bytes 393220

commit v2 on v1

--- a/solution.py
+++ b/solution.py
@@ -107,8 +107,8 @@
 
 def get_operands(t, spare):
     low = lane_index(C) < 64
-    even = spare[pl.ds(2 * t, C, 8), :]
-    odd = spare[pl.ds(2 * t + 1, C, 8), :]
+    even = spare[pl.ds(2 * t, C, 8), :].astype(BF16)
+    odd = spare[pl.ds(2 * t + 1, C, 8), :].astype(BF16)
     left = jnp.where(low, even, pltpu.roll(odd, 64, 1))
     right = jnp.where(low, pltpu.roll(even, 64, 1), odd)
     return left, right
@@ -128,8 +128,8 @@
         value = mm(proj_t[layer, pl.ds((base + 1) * C, C), :], normed, 1, 0)
         opened = jax.nn.sigmoid(closed)
         operand = opened * value * valid
-        fact_ref[pl.ds(base * C, C), wide(h)] = operand * (1.0 - opened)
-        fact_ref[pl.ds((base + 1) * C, C), wide(h)] = opened * valid
+        fact_ref[pl.ds(base * C, C), wide(h)] = (operand * (1.0 - opened)).astype(BF16)
+        fact_ref[pl.ds((base + 1) * C, C), wide(h)] = (opened * valid).astype(BF16)
         parts.append(operand)
     for t, piece in inner(h):
         put_operands(t, parts[0][:, piece], parts[1][:, piece], spare)
@@ -240,7 +240,7 @@
     d_left, d_right = get_operands(t, spare)
     for part, d_out in enumerate((d_left, d_left, d_right, d_right)):
         rows = pl.ds(part * C, C)
-        kept_p[rows, tile(t)] = (d_out * fact_ref[rows, tile(t)]).astype(BF16)
+        kept_p[rows, tile(t)] = d_out * fact_ref[rows, tile(t)]
 
 
 def both_back_kernel(
@@ -311,9 +311,9 @@
                 scale_ref[pl.ds(0, 1), tile(t)],
             )
             outs.append(grad_ref[:, tile(t)] + d_x)
-    weights = mm(normed_ref[...], kept_p[...], 1, 1)
+    normed = normed_ref[...]
     for e in range(4):
-        spare[pl.ds(e, C, 8), :] = weights[:, e * C : (e + 1) * C]
+        spare[pl.ds(e, C, 8), :] = mm(normed, kept_p[tile(e), :], 1, 1)
         spare[pl.ds(4 + e, C, 8), :] = keep_ref[e]
     send_ref[...] = spare[...].astype(BF16)
     lanes_to_pairs(outs, pair_grad_ref, pairs)
@@ -426,7 +426,11 @@
 
 
 def collect_kernel(recv_ref, sums_ref, send_ref):
-    total = jnp.sum(recv_ref[...].astype(F32).reshape(PEERS, 8, LANES), axis=0)
+    parts = recv_ref[...].astype(F32).reshape(PEERS, 8, LANES)
+    while parts.shape[0] > 1:
+        middle = parts.shape[0] // 2
+        parts = parts[:middle] + parts[middle:]
+    total = parts[0]
     block = [total[0:4], sums_ref[...], total[4:8]]
     both = jnp.concatenate(block + block, axis=0)
     send_ref[...] = (
@@ -513,7 +517,7 @@
     half = ((2, TOKENS, LANES), F32)
     pair_shape = ((ROWS, COLS, C), BF16)
 
-    saved = [plane, scales, plane_b, (four, F32), plane, plane_b]
+    saved = [plane, scales, plane_b, (four, BF16), plane, plane_b]
     places = run(place_kernel, [((TOKENS, PLACE), BF16)] * 2, [], ())
     (
         send, unit0, scale0, normed0, fact0, gating0, x0,

time: 167 us -> 167 us (level)
  no operation moved by 1% of the time
where the time goes in v2:
time: 167 us; the launch traced here: 166 us
  blocking collectives  157 us (94%)
  Pallas kernels  7.6 us (5%)
    all_to_all x10, blocking collectives, exchange(): lax.all_to_all(values.reshape(-1, rows, LANES), AXES, 0, 0, tiled=True)  157 us
    pallas_call x12, Pallas kernels, run(): pl.pallas_call(kernel, out_shape=[jax.ShapeDtypeStruct(shape, dtype) for...  7.6 us

profile of v2, /device:TPU:1, one launch (start us, length us, event | category | flops | bytes accessed | tf_op | source)
XLA Modules:
  0.0 166.2 jit_solution(14450448279663950788)
XLA Ops:
  0.6 0.0 copy-start.4
  0.6 0.0 copy-start.3
  0.7 0.0 copy-start
  0.7 0.0 copy-start.1
  0.7 0.1 shard_map.135
  0.8 0.0 copy-start.5
  0.8 0.7 copy-done.4
  1.5 0.0 copy-done.3
  1.5 0.2 copy-done
  1.7 0.0 copy-done.1
  1.7 0.7 shard_map.136
  2.4 22.8 %all_to_all.50 = bf16[128,8,128]{2,1,0:T(8,128)(2,1)S(1)} all-to-all(bf16[128,8,128]{2,1,0:T(8,128)(2,1)S(1)} %bitcast.25), channel_id=1, replica_groups=mesh['row'=8,'col'=16] {'row','col'}, dimensions={0} | all-to-all | bytes 524288 | tf_op jit(solution)/shard_map/all_to_all | solution.py:500
  25.2 0.6 shard_map.137
  25.8 14.1 %all_to_all.51 = bf16[128,4,128]{2,1,0:T(4,128)(2,1)S(1)} all-to-all(bf16[128,4,128]{2,1,0:T(4,128)(2,1)S(1)} %bitcast.38), channel_id=1, replica_groups=mesh['row'=8,'col'=16] {'row','col'}, dimensions={0} | all-to-all | bytes 262144 | tf_op jit(solution)/shard_map/all_to_all | solution.py:500
  39.9 0.8 shard_map.138
  40.7 15.0 %all_to_all.52 = bf16[128,8,128]{2,1,0:T(8,128)(2,1)S(1)} all-to-all(bf16[128,8,128]{2,1,0:T(8,128)(2,1)S(1)} %bitcast.26), channel_id=1, replica_groups=mesh['row'=8,'col'=16] {'row','col'}, dimensions={0} | all-to-all | bytes 524288 | tf_op jit(solution)/shard_map/all_to_all | solution.py:500
  55.7 0.6 shard_map.139
  56.3 0.0 copy-start.2
  56.4 14.1 %all_to_all.53 = bf16[128,4,128]{2,1,0:T(4,128)(2,1)S(1)} all-to-all(bf16[128,4,128]{2,1,0:T(4,128)(2,1)S(1)} %bitcast.39), channel_id=1, replica_groups=mesh['row'=8,'col'=16] {'row','col'}, dimensions={0} | all-to-all | bytes 262144 | tf_op jit(solution)/shard_map/all_to_all | solution.py:500
  70.5 0.7 shard_map.140
  71.2 14.0 %all_to_all.54 = bf16[128,4,128]{2,1,0:T(4,128)(2,1)S(1)} all-to-all(bf16[128,4,128]{2,1,0:T(4,128)(2,1)S(1)} %bitcast.37), channel_id=1, replica_groups=mesh['row'=8,'col'=16] {'row','col'}, dimensions={0} | all-to-all | bytes 262144 | tf_op jit(solution)/shard_map/all_to_all | solution.py:500
  85.2 0.6 shard_map.141
  85.8 15.0 %all_to_all.55 = bf16[128,8,128]{2,1,0:T(8,128)(2,1)S(1)} all-to-all(bf16[128,8,128]{2,1,0:T(8,128)(2,1)S(1)} %bitcast.33), channel_id=1, replica_groups=mesh['row'=8,'col'=16] {'row','col'}, dimensions={0} | all-to-all | bytes 524288 | tf_op jit(solution)/shard_map/all_to_all | solution.py:500
  100.8 1.0 shard_map.142
  101.8 15.1 %all_to_all.56 = bf16[128,8,128]{2,1,0:T(8,128)(2,1)S(1)} all-to-all(bf16[128,8,128]{2,1,0:T(8,128)(2,1)S(1)} %bitcast.24), channel_id=1, replica_groups=mesh['row'=8,'col'=16] {'row','col'}, dimensions={0} | all-to-all | bytes 524288 | tf_op jit(solution)/shard_map/all_to_all | solution.py:500
  117.0 0.7 shard_map.143
  117.6 15.1 %all_to_all.57 = bf16[128,8,128]{2,1,0:T(8,128)(2,1)S(1)} all-to-all(bf16[128,8,128]{2,1,0:T(8,128)(2,1)S(1)} %bitcast.30), channel_id=1, replica_groups=mesh['row'=8,'col'=16] {'row','col'}, dimensions={0} | all-to-all | bytes 524288 | tf_op jit(solution)/shard_map/all_to_all | solution.py:500
  132.8 0.7 shard_map.144
  133.5 15.1 %all_to_all.58 = bf16[128,8,128]{2,1,0:T(8,128)(2,1)S(1)} all-to-all(bf16[128,8,128]{2,1,0:T(8,128)(2,1)S(1)} %bitcast.28), channel_id=1, replica_groups=mesh['row'=8,'col'=16] {'row','col'}, dimensions={0} | all-to-all | bytes 524288 | tf_op jit(solution)/shard_map/all_to_all | solution.py:500
  148.6 0.1 shard_map.145
  148.7 16.5 %all_to_all.59 = bf16[384,4,128]{2,1,0:T(4,128)(2,1)S(1)} all-to-all(bf16[384,4,128]{2,1,0:T(4,128)(2,1)S(1)} %bitcast.22), channel_id=1, replica_groups=mesh['row'=8,'col'=16] {'row','col'}, dimensions={0} | all-to-all | bytes 786432 | tf_op jit(solution)/shard_map/all_to_all | solution.py:500
  165.1 1.1 shard_map.146
  (6 shorter events, 0.0 us)
Async XLA Ops:
  0.6 0.8 copy-start.4
  0.6 0.9 copy-start.3
  0.7 1.0 copy-start
  0.7 1.0 copy-start.1
  0.7 1.0 copy-start.6
  0.7 1.0 copy-start.7
  0.8 0.9 copy-start.5
  56.3 14.1 %copy-start.2 = (bf16[32,16,128]{2,1,0:T(8,128)(2,1)S(1)}, bf16[32,16,128]{2,1,0:T(8,128)(2,1)}, u32[]{:S(2)}) copy-start(bf16[32,16,128]{2,1,0:T(8,128)(2,1)} %cot_ref.1) | copy-start | bytes 393220

commit v3 on v1

--- a/solution.py
+++ b/solution.py
@@ -273,7 +273,7 @@
             kept_d[:, tile(t)] = (grad * gating_ref[:, tile(t)]).astype(BF16)
             kept_g[:, tile(t)] = (grad * gate_fact_ref[:, tile(t)]).astype(BF16)
         d_mid.append(mm(out_w[0], kept_d[:, wide(h)], 1, 0))
-    weights = mm(normed1_ref[...], kept_p[...], 1, 1)
+    normed1 = normed1_ref[...]
     for h in range(2):
         for t, piece in inner(h):
             spare[pl.ds(t, C, 8), :] = standardize_back(
@@ -281,7 +281,7 @@
                 mix_unit_ref[:, tile(t)],
                 mix_scale_ref[pl.ds(0, 1), tile(t)],
             )
-            spare[pl.ds(TILES + t, C, 8), :] = weights[:, t * LANES : (t + 1) * LANES]
+            spare[pl.ds(TILES + t, C, 8), :] = mm(normed1, kept_p[tile(t), :], 1, 1)
     d_gated_ref[...] = mm(gate[0], kept_g[...], 1, 0)
     send_ref[...] = spare[...].astype(BF16)
     keep_ref[0] = mm(normed0_ref[...], kept_g[...], 1, 1)
@@ -311,9 +311,9 @@
                 scale_ref[pl.ds(0, 1), tile(t)],
             )
             outs.append(grad_ref[:, tile(t)] + d_x)
-    weights = mm(normed_ref[...], kept_p[...], 1, 1)
+    normed = normed_ref[...]
     for e in range(4):
-        spare[pl.ds(e, C, 8), :] = weights[:, e * C : (e + 1) * C]
+        spare[pl.ds(e, C, 8), :] = mm(normed, kept_p[tile(e), :], 1, 1)
         spare[pl.ds(4 + e, C, 8), :] = keep_ref[e]
     send_ref[...] = spare[...].astype(BF16)
     lanes_to_pairs(outs, pair_grad_ref, pairs)
@@ -426,7 +426,11 @@
 
 
 def collect_kernel(recv_ref, sums_ref, send_ref):
-    total = jnp.sum(recv_ref[...].astype(F32).reshape(PEERS, 8, LANES), axis=0)
+    parts = recv_ref[...].astype(F32).reshape(PEERS, 8, LANES)
+    while parts.shape[0] > 1:
+        middle = parts.shape[0] // 2
+        parts = parts[:middle] + parts[middle:]
+    total = parts[0]
     block = [total[0:4], sums_ref[...], total[4:8]]
     both = jnp.concatenate(block + block, axis=0)
     send_ref[...] = (

time: 167 us -> 167 us (level)
  no operation moved by 1% of the time
where the time goes in v3:
time: 167 us; the launch traced here: 166 us
  blocking collectives  157 us (94%)
  Pallas kernels  7.72 us (5%)
    all_to_all x10, blocking collectives, exchange(): lax.all_to_all(values.reshape(-1, rows, LANES), AXES, 0, 0, tiled=True)  157 us
    pallas_call x12, Pallas kernels, run(): pl.pallas_call(kernel, out_shape=[jax.ShapeDtypeStruct(shape, dtype) for...  7.72 us

profile of v3, /device:TPU:1, one launch (start us, length us, event | category | flops | bytes accessed | tf_op | source)
XLA Modules:
  0.0 166.3 jit_solution(16827701151042637595)
XLA Ops:
  0.6 0.0 copy-start.4
  0.6 0.0 copy-start.3
  0.7 0.0 copy-start
  0.7 0.0 copy-start.1
  0.7 0.1 shard_map.135
  0.8 0.0 copy-start.5
  0.8 0.7 copy-done.4
  1.5 0.0 copy-done.3
  1.5 0.2 copy-done
  1.7 0.0 copy-done.1
  1.7 0.7 shard_map.136
  2.4 22.8 %all_to_all.50 = bf16[128,8,128]{2,1,0:T(8,128)(2,1)S(1)} all-to-all(bf16[128,8,128]{2,1,0:T(8,128)(2,1)S(1)} %bitcast.25), channel_id=1, replica_groups=mesh['row'=8,'col'=16] {'row','col'}, dimensions={0} | all-to-all | bytes 524288 | tf_op jit(solution)/shard_map/all_to_all | solution.py:500
  25.1 0.6 shard_map.137
  25.7 14.1 %all_to_all.51 = bf16[128,4,128]{2,1,0:T(4,128)(2,1)S(1)} all-to-all(bf16[128,4,128]{2,1,0:T(4,128)(2,1)S(1)} %bitcast.38), channel_id=1, replica_groups=mesh['row'=8,'col'=16] {'row','col'}, dimensions={0} | all-to-all | bytes 262144 | tf_op jit(solution)/shard_map/all_to_all | solution.py:500
  39.9 0.9 shard_map.138
  40.7 15.0 %all_to_all.52 = bf16[128,8,128]{2,1,0:T(8,128)(2,1)S(1)} all-to-all(bf16[128,8,128]{2,1,0:T(8,128)(2,1)S(1)} %bitcast.26), channel_id=1, replica_groups=mesh['row'=8,'col'=16] {'row','col'}, dimensions={0} | all-to-all | bytes 524288 | tf_op jit(solution)/shard_map/all_to_all | solution.py:500
  55.7 0.6 shard_map.139
  56.3 0.0 copy-start.2
  56.4 14.1 %all_to_all.53 = bf16[128,4,128]{2,1,0:T(4,128)(2,1)S(1)} all-to-all(bf16[128,4,128]{2,1,0:T(4,128)(2,1)S(1)} %bitcast.39), channel_id=1, replica_groups=mesh['row'=8,'col'=16] {'row','col'}, dimensions={0} | all-to-all | bytes 262144 | tf_op jit(solution)/shard_map/all_to_all | solution.py:500
  70.5 0.7 shard_map.140
  71.2 14.0 %all_to_all.54 = bf16[128,4,128]{2,1,0:T(4,128)(2,1)S(1)} all-to-all(bf16[128,4,128]{2,1,0:T(4,128)(2,1)S(1)} %bitcast.37), channel_id=1, replica_groups=mesh['row'=8,'col'=16] {'row','col'}, dimensions={0} | all-to-all | bytes 262144 | tf_op jit(solution)/shard_map/all_to_all | solution.py:500
  85.2 0.6 shard_map.141
  85.8 15.0 %all_to_all.55 = bf16[128,8,128]{2,1,0:T(8,128)(2,1)S(1)} all-to-all(bf16[128,8,128]{2,1,0:T(8,128)(2,1)S(1)} %bitcast.33), channel_id=1, replica_groups=mesh['row'=8,'col'=16] {'row','col'}, dimensions={0} | all-to-all | bytes 524288 | tf_op jit(solution)/shard_map/all_to_all | solution.py:500
  100.8 1.1 shard_map.142
  101.9 15.1 %all_to_all.56 = bf16[128,8,128]{2,1,0:T(8,128)(2,1)S(1)} all-to-all(bf16[128,8,128]{2,1,0:T(8,128)(2,1)S(1)} %bitcast.24), channel_id=1, replica_groups=mesh['row'=8,'col'=16] {'row','col'}, dimensions={0} | all-to-all | bytes 524288 | tf_op jit(solution)/shard_map/all_to_all | solution.py:500
  117.0 0.7 shard_map.143
  117.7 15.1 %all_to_all.57 = bf16[128,8,128]{2,1,0:T(8,128)(2,1)S(1)} all-to-all(bf16[128,8,128]{2,1,0:T(8,128)(2,1)S(1)} %bitcast.30), channel_id=1, replica_groups=mesh['row'=8,'col'=16] {'row','col'}, dimensions={0} | all-to-all | bytes 524288 | tf_op jit(solution)/shard_map/all_to_all | solution.py:500
  132.8 0.7 shard_map.144
  133.6 15.1 %all_to_all.58 = bf16[128,8,128]{2,1,0:T(8,128)(2,1)S(1)} all-to-all(bf16[128,8,128]{2,1,0:T(8,128)(2,1)S(1)} %bitcast.28), channel_id=1, replica_groups=mesh['row'=8,'col'=16] {'row','col'}, dimensions={0} | all-to-all | bytes 524288 | tf_op jit(solution)/shard_map/all_to_all | solution.py:500
  148.7 0.1 shard_map.145
  148.8 16.5 %all_to_all.59 = bf16[384,4,128]{2,1,0:T(4,128)(2,1)S(1)} all-to-all(bf16[384,4,128]{2,1,0:T(4,128)(2,1)S(1)} %bitcast.23), channel_id=1, replica_groups=mesh['row'=8,'col'=16] {'row','col'}, dimensions={0} | all-to-all | bytes 786432 | tf_op jit(solution)/shard_map/all_to_all | solution.py:500
  165.2 1.1 shard_map.146
  (6 shorter events, 0.0 us)
Async XLA Ops:
  0.6 0.8 copy-start.4
  0.6 0.9 copy-start.3
  0.7 1.0 copy-start
  0.7 1.0 copy-start.1
  0.7 1.0 copy-start.6
  0.7 1.0 copy-start.7
  0.8 0.9 copy-start.5
  56.3 14.1 %copy-start.2 = (bf16[32,16,128]{2,1,0:T(8,128)(2,1)S(1)}, bf16[32,16,128]{2,1,0:T(8,128)(2,1)}, u32[]{:S(2)}) copy-start(bf16[32,16,128]{2,1,0:T(8,128)(2,1)} %cot_ref.1) | copy-start | bytes 393220

commit v4 on v3

--- a/solution.py
+++ b/solution.py
@@ -105,10 +105,10 @@
     spare[pl.ds(2 * t + 1, C, 8), :] = jnp.where(low, pltpu.roll(left, 64, 1), right)
 
 
-def get_operands(t, spare):
+def get_operands(t, spare, dtype):
     low = lane_index(C) < 64
-    even = spare[pl.ds(2 * t, C, 8), :]
-    odd = spare[pl.ds(2 * t + 1, C, 8), :]
+    even = spare[pl.ds(2 * t, C, 8), :].astype(dtype)
+    odd = spare[pl.ds(2 * t + 1, C, 8), :].astype(dtype)
     left = jnp.where(low, even, pltpu.roll(odd, 64, 1))
     right = jnp.where(low, pltpu.roll(even, 64, 1), odd)
     return left, right
@@ -128,8 +128,8 @@
         value = mm(proj_t[layer, pl.ds((base + 1) * C, C), :], normed, 1, 0)
         opened = jax.nn.sigmoid(closed)
         operand = opened * value * valid
-        fact_ref[pl.ds(base * C, C), wide(h)] = operand * (1.0 - opened)
-        fact_ref[pl.ds((base + 1) * C, C), wide(h)] = opened * valid
+        fact_ref[pl.ds(base * C, C), wide(h)] = (operand * (1.0 - opened)).astype(fact_ref.dtype)
+        fact_ref[pl.ds((base + 1) * C, C), wide(h)] = (opened * valid).astype(fact_ref.dtype)
         parts.append(operand)
     for t, piece in inner(h):
         put_operands(t, parts[0][:, piece], parts[1][:, piece], spare)
@@ -237,7 +237,7 @@
 
 
 def projected_back(t, spare, fact_ref, kept_p):
-    d_left, d_right = get_operands(t, spare)
+    d_left, d_right = get_operands(t, spare, fact_ref.dtype)
     for part, d_out in enumerate((d_left, d_left, d_right, d_right)):
         rows = pl.ds(part * C, C)
         kept_p[rows, tile(t)] = (d_out * fact_ref[rows, tile(t)]).astype(BF16)
@@ -517,7 +517,8 @@
     half = ((2, TOKENS, LANES), F32)
     pair_shape = ((ROWS, COLS, C), BF16)
 
-    saved = [plane, scales, plane_b, (four, F32), plane, plane_b]
+    saved0 = [plane, scales, plane_b, (four, BF16), plane, plane_b]
+    saved1 = [plane, scales, plane_b, (four, F32), plane, plane_b]
     places = run(place_kernel, [((TOKENS, PLACE), BF16)] * 2, [], ())
     (
         send, unit0, scale0, normed0, fact0, gating0, x0,
@@ -525,7 +526,7 @@
     ) = run(
         first_kernel,
         [operand]
-        + saved
+        + saved0
         + [(a.shape, a.dtype) for a in (proj_w, gate_w, out_w, gain_in, gain_mid)]
         + [((2, 4 * C, C), BF16), ((2, C, C), BF16), ((2, C, C), BF16)]
         + [scales],
@@ -540,7 +541,7 @@
         send, unit1, scale1, normed1, fact1, gating1, x1,
         mix_unit0, mix_scale0, mix_normed0, gate_fact0,
     ) = run(
-        middle_kernel, [operand] + saved + [plane, scales, plane_b, plane], [spare, mixed],
+        middle_kernel, [operand] + saved1 + [plane, scales, plane_b, plane], [spare, mixed],
         (exchange(send, 4), x0, gating0, valid, gin, gmid, proj_t, gate_t, out_t),
     )
     send, left1, right1 = run(

time: 167 us -> 167 us (level)
  no operation moved by 1% of the time
where the time goes in v4:
time: 167 us; the launch traced here: 166 us
  blocking collectives  157 us (94%)
  Pallas kernels  7.66 us (5%)
    all_to_all x10, blocking collectives, exchange(): lax.all_to_all(values.reshape(-1, rows, LANES), AXES, 0, 0, tiled=True)  157 us
    pallas_call x12, Pallas kernels, run(): pl.pallas_call(kernel, out_shape=[jax.ShapeDtypeStruct(shape, dtype) for...  7.66 us

profile of v4, /device:TPU:1, one launch (start us, length us, event | category | flops | bytes accessed | tf_op | source)
XLA Modules:
  0.0 166.2 jit_solution(2067096416926474499)
XLA Ops:
  0.6 0.0 copy-start.4
  0.6 0.0 copy-start.3
  0.7 0.0 copy-start
  0.7 0.0 copy-start.1
  0.7 0.1 shard_map.135
  0.8 0.0 copy-start.5
  0.8 0.7 copy-done.4
  1.5 0.0 copy-done.3
  1.5 0.2 copy-done
  1.7 0.0 copy-done.1
  1.7 0.7 shard_map.136
  2.4 22.8 %all_to_all.50 = bf16[128,8,128]{2,1,0:T(8,128)(2,1)S(1)} all-to-all(bf16[128,8,128]{2,1,0:T(8,128)(2,1)S(1)} %bitcast.25), channel_id=1, replica_groups=mesh['row'=8,'col'=16] {'row','col'}, dimensions={0} | all-to-all | bytes 524288 | tf_op jit(solution)/shard_map/all_to_all | solution.py:500
  25.2 0.6 shard_map.137
  25.8 14.1 %all_to_all.51 = bf16[128,4,128]{2,1,0:T(4,128)(2,1)S(1)} all-to-all(bf16[128,4,128]{2,1,0:T(4,128)(2,1)S(1)} %bitcast.38), channel_id=1, replica_groups=mesh['row'=8,'col'=16] {'row','col'}, dimensions={0} | all-to-all | bytes 262144 | tf_op jit(solution)/shard_map/all_to_all | solution.py:500
  39.9 0.9 shard_map.138
  40.7 15.0 %all_to_all.52 = bf16[128,8,128]{2,1,0:T(8,128)(2,1)S(1)} all-to-all(bf16[128,8,128]{2,1,0:T(8,128)(2,1)S(1)} %bitcast.26), channel_id=1, replica_groups=mesh['row'=8,'col'=16] {'row','col'}, dimensions={0} | all-to-all | bytes 524288 | tf_op jit(solution)/shard_map/all_to_all | solution.py:500
  55.8 0.6 shard_map.139
  56.4 0.0 copy-start.2
  56.4 14.1 %all_to_all.53 = bf16[128,4,128]{2,1,0:T(4,128)(2,1)S(1)} all-to-all(bf16[128,4,128]{2,1,0:T(4,128)(2,1)S(1)} %bitcast.39), channel_id=1, replica_groups=mesh['row'=8,'col'=16] {'row','col'}, dimensions={0} | all-to-all | bytes 262144 | tf_op jit(solution)/shard_map/all_to_all | solution.py:500
  70.5 0.7 shard_map.140
  71.2 14.0 %all_to_all.54 = bf16[128,4,128]{2,1,0:T(4,128)(2,1)S(1)} all-to-all(bf16[128,4,128]{2,1,0:T(4,128)(2,1)S(1)} %bitcast.37), channel_id=1, replica_groups=mesh['row'=8,'col'=16] {'row','col'}, dimensions={0} | all-to-all | bytes 262144 | tf_op jit(solution)/shard_map/all_to_all | solution.py:500
  85.2 0.6 shard_map.141
  85.8 15.0 %all_to_all.55 = bf16[128,8,128]{2,1,0:T(8,128)(2,1)S(1)} all-to-all(bf16[128,8,128]{2,1,0:T(8,128)(2,1)S(1)} %bitcast.33), channel_id=1, replica_groups=mesh['row'=8,'col'=16] {'row','col'}, dimensions={0} | all-to-all | bytes 524288 | tf_op jit(solution)/shard_map/all_to_all | solution.py:500
  100.8 1.0 shard_map.142
  101.9 15.1 %all_to_all.56 = bf16[128,8,128]{2,1,0:T(8,128)(2,1)S(1)} all-to-all(bf16[128,8,128]{2,1,0:T(8,128)(2,1)S(1)} %bitcast.24), channel_id=1, replica_groups=mesh['row'=8,'col'=16] {'row','col'}, dimensions={0} | all-to-all | bytes 524288 | tf_op jit(solution)/shard_map/all_to_all | solution.py:500
  117.0 0.7 shard_map.143
  117.7 15.1 %all_to_all.57 = bf16[128,8,128]{2,1,0:T(8,128)(2,1)S(1)} all-to-all(bf16[128,8,128]{2,1,0:T(8,128)(2,1)S(1)} %bitcast.30), channel_id=1, replica_groups=mesh['row'=8,'col'=16] {'row','col'}, dimensions={0} | all-to-all | bytes 524288 | tf_op jit(solution)/shard_map/all_to_all | solution.py:500
  132.8 0.7 shard_map.144
  133.5 15.1 %all_to_all.58 = bf16[128,8,128]{2,1,0:T(8,128)(2,1)S(1)} all-to-all(bf16[128,8,128]{2,1,0:T(8,128)(2,1)S(1)} %bitcast.28), channel_id=1, replica_groups=mesh['row'=8,'col'=16] {'row','col'}, dimensions={0} | all-to-all | bytes 524288 | tf_op jit(solution)/shard_map/all_to_all | solution.py:500
  148.7 0.1 shard_map.145
  148.7 16.5 %all_to_all.59 = bf16[384,4,128]{2,1,0:T(4,128)(2,1)S(1)} all-to-all(bf16[384,4,128]{2,1,0:T(4,128)(2,1)S(1)} %bitcast.23), channel_id=1, replica_groups=mesh['row'=8,'col'=16] {'row','col'}, dimensions={0} | all-to-all | bytes 786432 | tf_op jit(solution)/shard_map/all_to_all | solution.py:500
  165.2 1.1 shard_map.146
  (6 shorter events, 0.0 us)
Async XLA Ops:
  0.6 0.8 copy-start.4
  0.6 0.9 copy-start.3
  0.7 1.0 copy-start
  0.7 1.0 copy-start.1
  0.7 1.0 copy-start.6
  0.7 1.0 copy-start.7
  0.8 0.9 copy-start.5
  56.4 14.1 %copy-start.2 = (bf16[32,16,128]{2,1,0:T(8,128)(2,1)S(1)}, bf16[32,16,128]{2,1,0:T(8,128)(2,1)}, u32[]{:S(2)}) copy-start(bf16[32,16,128]{2,1,0:T(8,128)(2,1)} %cot_ref.1) | copy-start | bytes 393220

commit v5 on v4

--- a/solution.py
+++ b/solution.py
@@ -217,7 +217,7 @@
         for t, _ in inner(h):
             units.append(standardize(mixed[pl.ds(t, C, TILES), :]))
             kept_n[:, tile(t)] = (units[t][0] * gain).astype(BF16)
-            grad_ref[:, tile(t)] = cot[t]
+            grad_ref[:, tile(t)] = cot[t].astype(BF16)
             kept_d[:, tile(t)] = (cot[t] * gating_ref[:, tile(t)]).astype(BF16)
         d_normed.append(mm(out_w[1], kept_d[:, wide(h)], 1, 0))
         update.append(mm(out_t[1], kept_n[:, wide(h)], 1, 0))
@@ -268,7 +268,7 @@
                 unit_ref[:, tile(t)],
                 scale_ref[pl.ds(0, 1), tile(t)],
             )
-            grad = grad_ref[:, tile(t)] + d_x
+            grad = grad_ref[:, tile(t)].astype(F32) + d_x
             next_grad_ref[:, tile(t)] = grad
             kept_d[:, tile(t)] = (grad * gating_ref[:, tile(t)]).astype(BF16)
             kept_g[:, tile(t)] = (grad * gate_fact_ref[:, tile(t)]).astype(BF16)
@@ -548,7 +548,7 @@
         incoming_kernel, [single, square, square], [half], (exchange(send, 8),)
     )
     ready_out, send, grad1, d_gated1, weights1 = run(
-        turn_kernel, [pair_shape, single, plane, plane, ((2, C, C), F32)],
+        turn_kernel, [pair_shape, single, plane_b, plane, ((2, C, C), F32)],
         [mixed, pairs, plane_b, plane_b, plane_b],
         (exchange(send, 4), x1, gating1, normed1, cotangent, gmid, gate, out, out_t),
     )

time: 167 us -> 167 us (level)
  no operation moved by 1% of the time
where the time goes in v5:
time: 167 us; the launch traced here: 166 us
  blocking collectives  157 us (94%)
  Pallas kernels  7.63 us (5%)
    all_to_all x10, blocking collectives, exchange(): lax.all_to_all(values.reshape(-1, rows, LANES), AXES, 0, 0, tiled=True)  157 us
    pallas_call x12, Pallas kernels, run(): pl.pallas_call(kernel, out_shape=[jax.ShapeDtypeStruct(shape, dtype) for...  7.63 us

profile of v5, /device:TPU:1, one launch (start us, length us, event | category | flops | bytes accessed | tf_op | source)
XLA Modules:
  0.0 166.2 jit_solution(13613055691179274742)
XLA Ops:
  0.6 0.0 copy-start.4
  0.6 0.0 copy-start.3
  0.7 0.0 copy-start
  0.7 0.1 shard_map.135
  0.8 0.0 copy-start.5
  0.8 0.7 copy-done.4
  1.5 0.0 copy-done.3
  1.5 0.2 copy-done
  1.7 0.0 copy-done.1
  1.7 0.7 shard_map.136
  2.4 22.8 %all_to_all.50 = bf16[128,8,128]{2,1,0:T(8,128)(2,1)S(1)} all-to-all(bf16[128,8,128]{2,1,0:T(8,128)(2,1)S(1)} %bitcast.25), channel_id=1, replica_groups=mesh['row'=8,'col'=16] {'row','col'}, dimensions={0} | all-to-all | bytes 524288 | tf_op jit(solution)/shard_map/all_to_all | solution.py:500
  25.2 0.6 shard_map.137
  25.8 14.1 %all_to_all.51 = bf16[128,4,128]{2,1,0:T(4,128)(2,1)S(1)} all-to-all(bf16[128,4,128]{2,1,0:T(4,128)(2,1)S(1)} %bitcast.38), channel_id=1, replica_groups=mesh['row'=8,'col'=16] {'row','col'}, dimensions={0} | all-to-all | bytes 262144 | tf_op jit(solution)/shard_map/all_to_all | solution.py:500
  39.9 0.9 shard_map.138
  40.7 15.0 %all_to_all.52 = bf16[128,8,128]{2,1,0:T(8,128)(2,1)S(1)} all-to-all(bf16[128,8,128]{2,1,0:T(8,128)(2,1)S(1)} %bitcast.26), channel_id=1, replica_groups=mesh['row'=8,'col'=16] {'row','col'}, dimensions={0} | all-to-all | bytes 524288 | tf_op jit(solution)/shard_map/all_to_all | solution.py:500
  55.8 0.6 shard_map.139
  56.4 0.0 copy-start.2
  56.4 14.1 %all_to_all.53 = bf16[128,4,128]{2,1,0:T(4,128)(2,1)S(1)} all-to-all(bf16[128,4,128]{2,1,0:T(4,128)(2,1)S(1)} %bitcast.39), channel_id=1, replica_groups=mesh['row'=8,'col'=16] {'row','col'}, dimensions={0} | all-to-all | bytes 262144 | tf_op jit(solution)/shard_map/all_to_all | solution.py:500
  70.5 0.0 copy-done.2
  70.5 0.7 shard_map.140
  71.2 14.0 %all_to_all.54 = bf16[128,4,128]{2,1,0:T(4,128)(2,1)S(1)} all-to-all(bf16[128,4,128]{2,1,0:T(4,128)(2,1)S(1)} %bitcast.37), channel_id=1, replica_groups=mesh['row'=8,'col'=16] {'row','col'}, dimensions={0} | all-to-all | bytes 262144 | tf_op jit(solution)/shard_map/all_to_all | solution.py:500
  85.2 0.6 shard_map.141
  85.8 15.0 %all_to_all.55 = bf16[128,8,128]{2,1,0:T(8,128)(2,1)S(1)} all-to-all(bf16[128,8,128]{2,1,0:T(8,128)(2,1)S(1)} %bitcast.33), channel_id=1, replica_groups=mesh['row'=8,'col'=16] {'row','col'}, dimensions={0} | all-to-all | bytes 524288 | tf_op jit(solution)/shard_map/all_to_all | solution.py:500
  100.8 1.0 shard_map.142
  101.8 15.1 %all_to_all.56 = bf16[128,8,128]{2,1,0:T(8,128)(2,1)S(1)} all-to-all(bf16[128,8,128]{2,1,0:T(8,128)(2,1)S(1)} %bitcast.24), channel_id=1, replica_groups=mesh['row'=8,'col'=16] {'row','col'}, dimensions={0} | all-to-all | bytes 524288 | tf_op jit(solution)/shard_map/all_to_all | solution.py:500
  117.0 0.7 shard_map.143
  117.7 15.1 %all_to_all.57 = bf16[128,8,128]{2,1,0:T(8,128)(2,1)S(1)} all-to-all(bf16[128,8,128]{2,1,0:T(8,128)(2,1)S(1)} %bitcast.30), channel_id=1, replica_groups=mesh['row'=8,'col'=16] {'row','col'}, dimensions={0} | all-to-all | bytes 524288 | tf_op jit(solution)/shard_map/all_to_all | solution.py:500
  132.8 0.7 shard_map.144
  133.5 15.1 %all_to_all.58 = bf16[128,8,128]{2,1,0:T(8,128)(2,1)S(1)} all-to-all(bf16[128,8,128]{2,1,0:T(8,128)(2,1)S(1)} %bitcast.28), channel_id=1, replica_groups=mesh['row'=8,'col'=16] {'row','col'}, dimensions={0} | all-to-all | bytes 524288 | tf_op jit(solution)/shard_map/all_to_all | solution.py:500
  148.6 0.1 shard_map.145
  148.7 16.5 %all_to_all.59 = bf16[384,4,128]{2,1,0:T(4,128)(2,1)S(1)} all-to-all(bf16[384,4,128]{2,1,0:T(4,128)(2,1)S(1)} %bitcast.23), channel_id=1, replica_groups=mesh['row'=8,'col'=16] {'row','col'}, dimensions={0} | all-to-all | bytes 786432 | tf_op jit(solution)/shard_map/all_to_all | solution.py:500
  165.2 1.1 shard_map.146
  (6 shorter events, 0.0 us)
Async XLA Ops:
  0.6 0.8 copy-start.4
  0.6 0.9 copy-start.3
  0.7 1.0 copy-start
  0.7 1.0 copy-start.1
  0.7 1.0 copy-start.6
  0.7 1.0 copy-start.7
  0.8 0.9 copy-start.5
  56.4 14.1 %copy-start.2 = (bf16[32,16,128]{2,1,0:T(8,128)(2,1)S(1)}, bf16[32,16,128]{2,1,0:T(8,128)(2,1)}, u32[]{:S(2)}) copy-start(bf16[32,16,128]{2,1,0:T(8,128)(2,1)} %cot_ref.1) | copy-start | bytes 393220
